TPU v7x, 32 devices: a whole 2x2x4 slice. The times are simulated.
32 devices in a mesh: dp: 8 (over y, x, core), head: 4 (over z).
Axes of the slice: x: 2, y: 2, z: 4, core: 2. Of those that a mesh axis runs over, the one named last changes fastest.
Arguments:
- text: bfloat16 [16, 2, 492, 768], P('dp', None, 'head'), may hold values from -6 to 6
- boundary: int32 [16, 2, 492], P('dp'), may hold values from 0 to 1, as said below
- reset: int32 [16, 2], P('dp'), may hold values 0 or 1
- memory_in: bfloat16 [16, 10, 768], P('dp'), may hold values from -6 to 6
- init_memory: bfloat16 [10, 768], P(None, ('dp', 'head')), may hold values from -6 to 6
- w_qkv: bfloat16 [768, 3, 768], P(None, None, 'head'), may hold values from -0.21875 to 0.21875
- b_qv: bfloat16 [2, 12, 64], P(None, 'head'), may hold values from -3 to 3
- w_out: bfloat16 [768, 768], P('head'), may hold values from -0.875 to 0.875
- w_in: bfloat16 [768, 3072], P(None, ('dp', 'head')), may hold values from -0.21875 to 0.21875
- w_back: bfloat16 [3072, 768], P(('dp', 'head')), may hold values from -0.109375 to 0.109375
- b_in: bfloat16 [3072], P(('dp', 'head')), may hold values from -3 to 3
- norm_gains: bfloat16 [2, 768], P(None, ('dp', 'head')), may hold values from 0.5 to 1.5
- biases: bfloat16 [4, 768], P(None, ('dp', 'head')), may hold values from -2 to 2
- cotangent: bfloat16 [16, 2, 512, 768], P('dp', None, 'head'), may hold values from -6 to 6
Outputs:
- activations: bfloat16 [16, 2, 512, 768], P('dp', None, 'head')
- d_text: bfloat16 [16, 2, 492, 768], P('dp', None, 'head')
- d_init: float32 [10, 768], P(None, ('dp', 'head'))
- d_w_qkv: float32 [768, 3, 768], P('dp', None, 'head')
- d_b_qv: float32 [2, 12, 64], P(None, 'head', 'dp')
- d_w_out: float32 [768, 768], P('head', 'dp')
- d_w_in: float32 [768, 3072], P(None, ('dp', 'head'))
- d_w_back: float32 [3072, 768], P(('dp', 'head'))
- d_b_in: float32 [3072], P(('dp', 'head'))
- d_norm_gains: float32 [2, 768], P(None, ('dp', 'head'))
- d_biases: float32 [4, 768], P(None, ('dp', 'head'))
Inputs may be any that keep to these rules, and one draw needn't show every extreme that they name: `boundary`: in each aligned block of 2 sequences, one is a single document (it has no document start in either segment), as the data loader pairs one long document with one packed sequence.
All inputs are finite; a program needn't handle non-finite values. No bound on the sum of `reset` on one device may be relied on, other than what follows from the above.
Results may differ from a plain program's by a relative error of at most 0.024.
Values may be sent and summed in bfloat16 or wider, within the bound.
A program may use at most 192 MiB of HBM per device.

v0:
```python
import jax
import jax.numpy as jnp
from jax import lax
from jax.sharding import PartitionSpec as P

HD = 64


def from_root(x, axis, root):
    mine = lax.axis_index(axis) == root
    return lax.psum(jnp.where(mine, x, jnp.zeros_like(x)), axis)


def layer_norm(values, gain_row, shift_row):
    center = values - jnp.mean(values, axis=-1, keepdims=True)
    spread = jnp.mean(center * center, axis=-1, keepdims=True)
    return center * lax.rsqrt(spread + 1e-05) * gain_row + shift_row


def gelu_tanh(values):
    return jax.nn.gelu(values, approximate=True)


def head_major(array, dim, dp_count, head_count):
    shape = array.shape
    size = shape[dim]
    split = array.reshape(
        shape[:dim] + (dp_count, head_count, size // (dp_count * head_count)) + shape[dim + 1 :]
    )
    return jnp.swapaxes(split, dim, dim + 1).reshape(shape)


def local(
    text,
    boundary,
    reset,
    memory_in,
    init_memory,
    w_qkv,
    b_qv,
    w_out,
    w_in,
    w_back,
    b_in,
    norm_gains,
    biases,
    cotangent,
):
    head_count = lax.axis_size("head")
    dp_count = lax.axis_size("dp")
    head_idx = lax.axis_index("head")
    batch_size = text.shape[0]
    width = text.shape[3]
    seg_rows = cotangent.shape[2]
    seg_len = seg_rows * head_count
    mem_rows = memory_in.shape[1]
    text_len = seg_len - 2 * mem_rows
    local_width = w_qkv.shape[2]
    local_heads = local_width // HD
    row_start = head_idx * seg_rows
    is_first = (head_idx == 0).astype(jnp.float32)
    is_final = (head_idx == head_count - 1).astype(jnp.float32)
    grad_dims = (1, 0, 0, 1, 1, 1)
    doc_ids = jnp.cumsum(boundary, axis=2)
    marks = jnp.full((batch_size, 2, mem_rows), -1, jnp.int32)
    labels = jnp.concatenate([marks, doc_ids, marks], axis=2)
    visible = (
        (labels[..., :, None] == labels[..., None, :])
        | (labels[..., :, None] < 0)
        | (labels[..., None, :] < 0)
    )
    bias_query = b_qv[0].reshape(local_width).astype(jnp.float32)
    bias_value = b_qv[1].reshape(local_width).astype(jnp.float32)
    shared = (
        lax.all_gather(w_in, ("dp", "head"), axis=1, tiled=True),
        lax.all_gather(w_back, ("dp", "head"), axis=0, tiled=True),
        lax.all_gather(b_in, ("dp", "head"), axis=0, tiled=True),
        lax.all_gather(norm_gains, ("dp", "head"), axis=1, tiled=True),
        lax.all_gather(biases, ("dp", "head"), axis=1, tiled=True),
        lax.all_gather(init_memory, ("dp", "head"), axis=1, tiled=True),
    )

    def fetch():
        return shared

    def attention_probs(query, key_rows, seg):
        scores = (
            jnp.einsum("sqhe,skhe->shqk", query, key_rows, preferred_element_type=jnp.float32)
            * 0.125
        )
        return jnp.where(visible[:, seg][:, None], scores, -1e30)

    def forward(seg, memory, ffn):
        w_in_all, w_back_all, b_in_all, gains_all, biases_all, unused = ffn
        gains_f = gains_all.astype(jnp.float32)
        biases_f = biases_all.astype(jnp.float32)
        local_text = lax.all_gather(text[:, seg], "head", axis=1, tiled=True)
        x_rows = jnp.concatenate([memory, local_text, memory], axis=1)
        mixed = jnp.einsum("srd,dce->srce", x_rows, w_qkv, preferred_element_type=jnp.float32)
        query = (
            (mixed[:, :, 0] + bias_query)
            .astype(jnp.bfloat16)
            .reshape(batch_size, seg_len, local_heads, HD)
        )
        key_rows = mixed[:, :, 1].astype(jnp.bfloat16).reshape(batch_size, seg_len, local_heads, HD)
        value = (
            (mixed[:, :, 2] + bias_value)
            .astype(jnp.bfloat16)
            .reshape(batch_size, seg_len, local_heads, HD)
        )
        masked = attention_probs(query, key_rows, seg)
        row_max = jnp.max(masked, axis=-1, keepdims=True)
        exp_terms = jnp.exp(masked - row_max)
        row_total = jnp.sum(exp_terms, axis=-1, keepdims=True)
        log_total = row_max + jnp.log(row_total)
        probs = (exp_terms / row_total).astype(jnp.bfloat16)
        attended = jnp.einsum("shqk,skhe->sqhe", probs, value, preferred_element_type=jnp.float32)
        attended = attended.astype(jnp.bfloat16).reshape(batch_size, seg_len, local_width)
        partial_out = jnp.einsum("srl,ld->srd", attended, w_out, preferred_element_type=jnp.float32)
        summed = lax.psum_scatter(
            partial_out.astype(jnp.bfloat16), "head", scatter_dimension=1, tiled=True
        ).astype(jnp.float32)
        own_rows = lax.dynamic_slice_in_dim(x_rows, row_start, seg_rows, 1).astype(jnp.float32)
        pre_norm = own_rows + summed + biases_f[1]
        hidden = layer_norm(pre_norm, gains_f[0], biases_f[0])
        hidden_low = hidden.astype(jnp.bfloat16)
        inner = jnp.einsum(
            "srd,df->srf", hidden_low, w_in_all, preferred_element_type=jnp.float32
        ) + b_in_all.astype(jnp.float32)
        active = gelu_tanh(inner).astype(jnp.bfloat16)
        outer = (
            jnp.einsum("srf,fd->srd", active, w_back_all, preferred_element_type=jnp.float32)
            + biases_f[2]
        )
        post_norm = hidden + outer
        result = layer_norm(post_norm, gains_f[1], biases_f[3])
        kept = (
            x_rows,
            query,
            key_rows,
            value,
            log_total,
            attended,
            pre_norm,
            hidden_low,
            inner,
            active,
            post_norm,
        )
        return (result, kept)

    def backward(seg, grad_out, kept, ffn):
        (
            x_rows,
            query,
            key_rows,
            value,
            log_total,
            attended,
            pre_norm,
            hidden_low,
            inner,
            active,
            post_norm,
        ) = kept
        w_in_all, w_back_all, b_in_all, gains_all, biases_all, unused = ffn
        gains_f = gains_all.astype(jnp.float32)
        biases_f = biases_all.astype(jnp.float32)
        unused_two, pull_two = jax.vjp(layer_norm, post_norm, gains_f[1], biases_f[3])
        grad_post, grad_gain_two, grad_shift_two = pull_two(grad_out)
        grad_outer = grad_post.astype(jnp.bfloat16)
        grad_ffn_bias = jnp.sum(grad_post, axis=(0, 1))
        grad_w_back = jnp.einsum(
            "srf,srd->fd", active, grad_outer, preferred_element_type=jnp.float32
        )
        grad_active = jnp.einsum(
            "srd,fd->srf", grad_outer, w_back_all, preferred_element_type=jnp.float32
        )
        unused_gelu, pull_gelu = jax.vjp(gelu_tanh, inner)
        grad_inner = pull_gelu(grad_active)[0].astype(jnp.bfloat16)
        grad_b_in = jnp.sum(grad_inner, axis=(0, 1), dtype=jnp.float32)
        grad_w_in = jnp.einsum(
            "srd,srf->df", hidden_low, grad_inner, preferred_element_type=jnp.float32
        )
        grad_hidden = grad_post + jnp.einsum(
            "srf,df->srd", grad_inner, w_in_all, preferred_element_type=jnp.float32
        )
        unused_one, pull_one = jax.vjp(layer_norm, pre_norm, gains_f[0], biases_f[0])
        grad_pre, grad_gain_one, grad_shift_one = pull_one(grad_hidden)
        grad_out_bias = jnp.sum(grad_pre, axis=(0, 1))
        grad_branch = lax.all_gather(grad_pre.astype(jnp.bfloat16), "head", axis=1, tiled=True)
        grad_w_out = jnp.einsum(
            "srl,srd->ld", attended, grad_branch, preferred_element_type=jnp.float32
        )
        grad_att = jnp.einsum("srd,ld->srl", grad_branch, w_out, preferred_element_type=jnp.float32)
        grad_att = grad_att.astype(jnp.bfloat16).reshape(batch_size, seg_len, local_heads, HD)
        masked = attention_probs(query, key_rows, seg)
        probs = jnp.exp(masked - log_total)
        grad_value = jnp.einsum(
            "shqk,sqhe->skhe",
            probs.astype(jnp.bfloat16),
            grad_att,
            preferred_element_type=jnp.float32,
        )
        grad_probs = jnp.einsum(
            "sqhe,skhe->shqk", grad_att, value, preferred_element_type=jnp.float32
        )
        grad_scores = probs * (grad_probs - jnp.sum(grad_probs * probs, axis=-1, keepdims=True))
        grad_scores = grad_scores.astype(jnp.bfloat16)
        grad_query = (
            jnp.einsum("shqk,skhe->sqhe", grad_scores, key_rows, preferred_element_type=jnp.float32)
            * 0.125
        )
        grad_key = (
            jnp.einsum("shqk,sqhe->skhe", grad_scores, query, preferred_element_type=jnp.float32)
            * 0.125
        )
        grad_mixed = jnp.stack([grad_query, grad_key, grad_value], axis=2).astype(jnp.bfloat16)
        grad_mixed = grad_mixed.reshape(batch_size, seg_len, 3, local_width)
        grad_bias_qv = jnp.stack(
            [
                jnp.sum(grad_mixed[:, :, 0], axis=(0, 1), dtype=jnp.float32),
                jnp.sum(grad_mixed[:, :, 2], axis=(0, 1), dtype=jnp.float32),
            ]
        ).reshape(2, local_heads, HD)
        grad_w_qkv = jnp.einsum(
            "srd,srce->dce", x_rows, grad_mixed, preferred_element_type=jnp.float32
        )
        grad_rows = jnp.einsum(
            "srce,dce->srd", grad_mixed, w_qkv, preferred_element_type=jnp.float32
        )
        placed = lax.dynamic_update_slice_in_dim(jnp.zeros_like(grad_rows), grad_pre, row_start, 1)
        grad_rows = grad_rows + placed
        grad_text_part = lax.psum_scatter(
            grad_rows[:, mem_rows : mem_rows + text_len].astype(jnp.bfloat16),
            "head",
            scatter_dimension=1,
            tiled=True,
        ).astype(jnp.float32)
        grad_memory = lax.psum(
            (grad_rows[:, :mem_rows] + grad_rows[:, seg_len - mem_rows :]).astype(jnp.bfloat16),
            "head",
        ).astype(jnp.float32)
        reset_flag = reset[:, seg] > 0
        grad_init = (
            jnp.sum(jnp.where(reset_flag[:, None, None], grad_memory, 0.0), axis=0) * is_first
        )
        ffn_grads = (
            grad_w_in,
            grad_w_back,
            grad_b_in,
            jnp.stack([grad_gain_one, grad_gain_two]),
            jnp.stack([grad_shift_one, grad_out_bias, grad_ffn_bias, grad_shift_two]),
            grad_init,
        )
        return (grad_text_part, grad_memory, (grad_w_qkv, grad_bias_qv, grad_w_out), ffn_grads)

    ffn_first = fetch()
    init_all = ffn_first[5]
    memory_one = jnp.where(reset[:, 0, None, None] > 0, init_all[None], memory_in)
    out_one, kept_one = forward(0, memory_one, ffn_first)
    tail_rows = out_one[:, seg_rows - mem_rows :].astype(jnp.bfloat16)
    carried = from_root(tail_rows, "head", head_count - 1)
    ffn_second = fetch()
    memory_two = jnp.where(reset[:, 1, None, None] > 0, ffn_second[5][None], carried)
    out_two, kept_two = forward(1, memory_two, ffn_second)
    activations = jnp.stack([out_one, out_two], axis=1).astype(jnp.bfloat16)
    ffn_third = fetch()
    text_two, memory_grad_two, attn_two, ffn_two = backward(
        1, cotangent[:, 1].astype(jnp.float32), kept_two, ffn_third
    )
    keep_flag = reset[:, 1, None, None] <= 0
    carried_grad = jnp.where(keep_flag, memory_grad_two, 0.0) * is_final
    grad_one = cotangent[:, 0].astype(jnp.float32) + jnp.concatenate(
        [jnp.zeros((batch_size, seg_rows - mem_rows, width), jnp.float32), carried_grad], axis=1
    )
    ffn_fourth = fetch()
    text_one, memory_grad_one, attn_one, ffn_one = backward(0, grad_one, kept_one, ffn_fourth)
    grads = jax.tree.map(lambda a, b: a + b, ffn_one, ffn_two)
    ffn_total = tuple((head_major(g, d, dp_count, head_count) for g, d in zip(grads, grad_dims)))
    partial_sums = (
        lax.psum_scatter(
            ffn_total[0].astype(jnp.bfloat16), "head", scatter_dimension=1, tiled=True
        ).astype(jnp.float32),
        lax.psum_scatter(
            ffn_total[1].astype(jnp.bfloat16), "head", scatter_dimension=0, tiled=True
        ).astype(jnp.float32),
        lax.psum_scatter(
            ffn_total[2].astype(jnp.bfloat16), "head", scatter_dimension=0, tiled=True
        ).astype(jnp.float32),
        lax.psum_scatter(
            ffn_total[3].astype(jnp.bfloat16), "head", scatter_dimension=1, tiled=True
        ).astype(jnp.float32),
        lax.psum_scatter(
            ffn_total[4].astype(jnp.bfloat16), "head", scatter_dimension=1, tiled=True
        ).astype(jnp.float32),
        lax.psum_scatter(
            ffn_total[5].astype(jnp.bfloat16), "head", scatter_dimension=1, tiled=True
        ).astype(jnp.float32),
    )
    reduced = (
        lax.psum_scatter(partial_sums[0], "dp", scatter_dimension=1, tiled=True),
        lax.psum_scatter(partial_sums[1], "dp", scatter_dimension=0, tiled=True),
        lax.psum_scatter(partial_sums[2], "dp", scatter_dimension=0, tiled=True),
        lax.psum_scatter(partial_sums[3], "dp", scatter_dimension=1, tiled=True),
        lax.psum_scatter(partial_sums[4], "dp", scatter_dimension=1, tiled=True),
        lax.psum_scatter(partial_sums[5], "dp", scatter_dimension=1, tiled=True),
    )
    attn_total = jax.tree.map(lambda a, b: a + b, attn_one, attn_two)
    grad_qkv, grad_bqv, grad_wout = (
        lax.psum_scatter(attn_total[0], "dp", scatter_dimension=0, tiled=True),
        lax.psum_scatter(attn_total[1], "dp", scatter_dimension=2, tiled=True),
        lax.psum_scatter(attn_total[2], "dp", scatter_dimension=1, tiled=True),
    )
    grad_text = jnp.stack([text_one, text_two], axis=1).astype(jnp.bfloat16)
    grad_win, grad_wback, grad_bin, grad_gains, grad_biases, grad_init = reduced
    return (
        activations,
        grad_text,
        grad_init,
        grad_qkv,
        grad_bqv,
        grad_wout,
        grad_win,
        grad_wback,
        grad_bin,
        grad_gains,
        grad_biases,
    )


def solution(mesh):
    return jax.shard_map(
        local,
        mesh=mesh,
        in_specs=(
            P("dp", None, "head", None),
            P("dp", None, None),
            P("dp", None),
            P("dp", None, None),
            P(None, ("dp", "head")),
            P(None, None, "head"),
            P(None, "head", None),
            P("head", None),
            P(None, ("dp", "head")),
            P(("dp", "head"), None),
            P(("dp", "head")),
            P(None, ("dp", "head")),
            P(None, ("dp", "head")),
            P("dp", None, "head", None),
        ),
        out_specs=(
            P("dp", None, "head", None),
            P("dp", None, "head", None),
            P(None, ("dp", "head")),
            P("dp", None, "head"),
            P(None, "head", "dp"),
            P("head", "dp"),
            P(None, ("dp", "head")),
            P(("dp", "head"), None),
            P(("dp", "head")),
            P(None, ("dp", "head")),
            P(None, ("dp", "head")),
        ),
        check_vma=False,
    )
```

profile of v0, /device:TPU:0, one launch (start us, length us, event | category | flops | bytes accessed | tf_op | source)
XLA Modules:
  0.0 1043.6 jit_solution(13577948018777265545)
XLA Ops:
  7.3 2.7 fusion.149
  15.2 73.0 %all-gather.2 = bf16[32,24,10]{1,2,0:T(8,128)(2,1)S(1)} all-gather(bf16[1,24,10]{1,2,0:T(8,128)(2,1)S(1)} %bitcast.368), channel_id=1, replica_groups=mesh['dp'=8,'head'=4] {'dp','head'}, dimensions={0}, use_global_device_ids=true | all-gather | bytes 15840 | tf_op jit(solution)/shard_map/all_gather | solution.py:80
  96.0 1.7 copy-done.1
  99.0 1.8 convolution_convert_fusion.1
  102.3 39.9 %all-reduce.2 = bf16[3072]{0:T(1024)(128)(2,1)S(1)} all-reduce(bf16[3072]{0:T(1024)(128)(2,1)S(1)} %dynamic-update-slice.2), channel_id=1, replica_groups=mesh['dp'=8,'head'=4] {'dp','head'}, use_global_device_ids=true, to_apply=%add.2 | all-reduce | flops 3072 | bytes 12288
  142.2 65.3 %all-gather.4 = bf16[32,24,2]{1,2,0:T(2,128)(2,1)S(1)} all-gather(bf16[1,24,2]{1,2,0:T(2,128)(2,1)S(1)} %bitcast.370), channel_id=1, replica_groups=mesh['dp'=8,'head'=4] {'dp','head'}, dimensions={0}, use_global_device_ids=true | all-gather | bytes 3168 | tf_op jit(solution)/shard_map/all_gather | solution.py:78
  207.8 64.0 %all-gather.3 = bf16[32,24,4]{1,2,0:T(4,128)(2,1)S(1)} all-gather(bf16[1,24,4]{1,2,0:T(4,128)(2,1)S(1)} %bitcast.369), channel_id=1, replica_groups=mesh['dp'=8,'head'=4] {'dp','head'}, dimensions={0}, use_global_device_ids=true | all-gather | bytes 6336 | tf_op jit(solution)/shard_map/all_gather | solution.py:79
  272.7 2.7 copy.296
  275.4 1.8 pad_maximum_fusion
  280.1 5.9 fusion.22
  286.1 5.4 fusion.151
  292.1 18.4 %psum.21 = bf16[2,10,768]{2,1,0:T(8,128)(2,1)S(1)} all-reduce(bf16[2,10,768]{2,1,0:T(8,128)(2,1)S(1)} %slice_select_fusion), channel_id=1, replica_groups=mesh['dp'=8,'head'=4] {'head'}, use_global_device_ids=true, to_apply=%region_9.10 | all-reduce | flops 15360 | bytes 61440 | tf_op jit(solution)/shard_map/psum | solution.py:11
  310.5 2.5 fusion.55
  316.7 1.7 copy-done.2
  320.4 1.8 convolution_convert_fusion
  322.5 2.9 pad_maximum_fusion.1
  325.4 30.1 %reduce-scatter.26.cloned.1.call-done = bf16[2,128,768]{2,1,0:T(8,128)(2,1)} async-done(((bf16[2,512,768]{2,1,0:T(8,128)(2,1)}), bf16[2,128,768]{2,1,0:T(8,128)(2,1)}) %reduce-scatter.26.cloned.1.call-update) | async-done | bytes 393232 | tf_op jit(solution)/shard_map/reduce_scatter | solution.py:120
  358.5 4.2 fusion.25
  362.8 2.1 fusion.153
  367.3 4.7 convert_reduce_fusion
  372.1 2.1 multiply_reduce_fusion.2
  378.9 34.4 %all-gather.16.cloned.1.call-done = bf16[2,512,768]{2,1,0:T(8,128)(2,1)} async-done(((bf16[2,128,768]{2,1,0:T(8,128)(2,1)}), bf16[2,512,768]{2,1,0:T(8,128)(2,1)}) %all-gather.16.cloned.1.call-update) | async-done | bytes 1572880 | tf_op jit(solution)/shard_map/all_gather | solution.py:191
  413.3 2.1 convolution_convert_fusion.3
  415.5 4.8 fusion.86
  420.3 4.4 multiply_reduce_fusion.1
  424.7 1.8 multiply_convert_fusion.1
  432.4 18.6 %psum.22 = bf16[2,10,768]{2,1,0:T(8,128)(2,1)} all-reduce(bf16[2,10,768]{2,1,0:T(8,128)(2,1)} %fusion.121), channel_id=1, replica_groups=mesh['dp'=8,'head'=4] {'head'}, use_global_device_ids=true, to_apply=%region_22.23 | all-reduce | flops 15360 | bytes 61440 | tf_op jit(solution)/shard_map/psum | solution.py:240
  451.0 1.7 fusion.119
  452.6 1.7 multiply_reduce_fusion.3
  456.4 5.9 convert_reduce_fusion.1
  462.4 2.2 multiply_reduce_fusion.4
  467.5 4.3 fusion.115
  471.8 2.5 fusion
  474.3 2.6 copy.234
  477.6 3.4 fusion.125
  481.0 4.9 fusion.1
  485.9 6.6 copy.230
  492.5 4.9 copy.231
  515.9 2.0 convolution_bitcast_fusion.2
  518.0 2.1 convolution_convert_fusion.2
  520.1 4.0 fusion.83
  524.1 4.5 multiply_reduce_fusion
  528.7 1.9 multiply_convert_fusion
  535.8 21.2 %all-reduce.12 = (bf16[2,10,768]{2,1,0:T(8,128)(2,1)S(1)}, bf16[3072]{0:T(1024)(128)(2,1)S(1)}) all-reduce(bf16[2,10,768]{2,1,0:T(8,128)(2,1)S(1)} %fusion.120, bf16[3072]{0:T(1024)(128)(2,1)S(1)} %copy-done.91), channel_id=1, replica_groups=mesh['dp'=8,'head'=4] {'head'}, use_global_device_ids=true, to_apply=%region_30.31 | all-reduce | flops 18432 | bytes 73728 | tf_op jit(solution)/shard_map/psum | solution.py:240
  558.3 1.9 fusion.91
  561.5 2.2 slice.207
  563.6 2.3 copy.222
  565.9 2.1 slice.208
  568.1 2.3 copy.221
  570.8 2.8 fusion.57
  573.6 2.9 bitcast_add_fusion.2
  576.6 14.9 %reduce-scatter.34.cloned.1.call-done = bf16[768,768]{1,0:T(8,128)(2,1)} async-done(((bf16[3072,768]{1,0:T(8,128)(2,1)}), bf16[768,768]{1,0:T(8,128)(2,1)}) %reduce-scatter.34.cloned.1.call-update) | async-done | bytes 1179664 | tf_op jit(solution)/shard_map/reduce_scatter | solution.py:285
  591.5 2.9 convert_element_type.360
  594.5 85.0 %reduce-scatter.30.cloned.1.call-done = bf16[768,768]{0,1:T(8,128)(2,1)} async-done(((bf16[768,3072]{0,1:T(8,128)(2,1)}), bf16[768,768]{0,1:T(8,128)(2,1)}) %reduce-scatter.30.cloned.1.call-update) | async-done | bytes 1179664 | tf_op jit(solution)/shard_map/reduce_scatter | solution.py:282
  679.5 2.9 convert_element_type.355
  688.5 13.1 %reduce-scatter.42.cloned.1.call-done = bf16[192,2]{1,0:T(8,128)(2,1)} async-done(((bf16[768,2]{1,0:T(8,128)(2,1)}), bf16[192,2]{1,0:T(8,128)(2,1)}) %reduce-scatter.42.cloned.1.call-update) | async-done | bytes 784
  702.5 18.9 %reduce-scatter.44.cloned.1.call-done = bf16[192,4]{1,0:T(8,128)(2,1)} async-done(((bf16[768,4]{1,0:T(8,128)(2,1)}), bf16[192,4]{1,0:T(8,128)(2,1)}) %reduce-scatter.44.cloned.1.call-update) | async-done | bytes 1552
  722.9 18.4 %reduce-scatter.38.cloned.1.call-done = bf16[192,10]{1,0:T(8,128)(2,1)} async-done(((bf16[768,10]{1,0:T(8,128)(2,1)}), bf16[192,10]{1,0:T(8,128)(2,1)}) %reduce-scatter.38.cloned.1.call-update) | async-done | bytes 3856
  742.2 22.4 %all-reduce.11 = (f32[10,192]{1,0:T(8,128)S(1)}, f32[2,3,64]{2,1,0:T(4,128)S(1)}, f32[768]{0:T(1024)S(1)}, f32[2,192]{1,0:T(2,128)S(1)}, f32[4,192]{1,0:T(4,128)S(1)}) all-reduce(bf16[10,192]{1,0:T(8,128)(2,1)S(1)} %copy.264, f32[2,3,64]{2,1,0:T(4,128)S(1)} %maximum_add_fusion.2, ...), channel_id=9, replica_groups=mesh['dp'=8,'head'=4] {'dp'}, use_global_device_ids=true, to_apply=%region_34.35.clone | all-reduce | flops 4224 | bytes 27648
  767.8 10.1 reduce-scatter.40.cloned.1.call-done
  779.5 118.6 %all-reduce.16.cloned.1.call-done = (bf16[2,492,768]{2,0,1:T(2,128)(2,1)}, bf16[2,492,768]{2,0,1:T(2,128)(2,1)}) async-done(((bf16[2,492,768]{2,0,1:T(2,128)(2,1)}, bf16[2,492,768]{2,0,1:T(2,128)(2,1)}), (bf16[2,492,768]{2,0,1:T(2,128)(2,1)}, bf16[2,492,768]{2,0,1:T(2,128)(2,1)})) %all-reduce.16.cloned.1.call-update) | async-done | bytes 3022864
  903.1 40.3 %reduce-scatter.28.cloned.1.call-done = f32[96,3,192]{2,0,1:T(8,128)} async-done(((f32[768,3,192]{2,0,1:T(8,128)}), f32[96,3,192]{2,0,1:T(8,128)}) %reduce-scatter.28.cloned.1.call-update) | async-done | bytes 221200 | tf_op jit(solution)/shard_map/reduce_scatter | solution.py:311
  943.4 46.7 %reduce-scatter.36.cloned.1.call-done = f32[96,768]{1,0:T(8,128)} async-done(((f32[768,768]{1,0:T(8,128)}), f32[96,768]{1,0:T(8,128)}) %reduce-scatter.36.cloned.1.call-update) | async-done | bytes 294928 | tf_op jit(solution)/shard_map/reduce_scatter | solution.py:303
  990.0 46.3 %reduce-scatter.32.cloned.1.call-done = f32[768,96]{0,1:T(8,128)} async-done(((f32[768,768]{0,1:T(8,128)}), f32[768,96]{0,1:T(8,128)}) %reduce-scatter.32.cloned.1.call-update) | async-done | bytes 294928 | tf_op jit(solution)/shard_map/reduce_scatter | solution.py:302
  (455 shorter events, 89.4 us)
Async XLA Ops:
  7.2 85.1 %copy-start = (bf16[768,3,192]{0,2,1:T(8,128)(2,1)S(1)}, bf16[768,3,192]{0,2,1:T(8,128)(2,1)}, u32[]{:S(2)}) copy-start(bf16[768,3,192]{0,2,1:T(8,128)(2,1)} %param.19) | copy-start | bytes 2654212
  7.2 8.0 copy-start.115
  7.2 83.4 %all-gather.20.cloned.1.call-start = ((), (), s32[]{:S(2)}) async-start(), calls=%async_computation.22 | async-start | bytes 1889280 | tf_op jit(solution)/shard_map/all_gather | solution.py:97
  10.0 80.6 %copy-start.86 = (bf16[2,10,768]{2,0,1:T(2,128)(2,1)S(1)}, bf16[2,10,768]{2,0,1:T(2,128)(2,1)}, u32[]{:S(2)}) copy-start(bf16[2,10,768]{2,0,1:T(2,128)(2,1)} %param.17) | copy-start | bytes 92164
  11.2 261.5 %all-gather.22.cloned.1.call-start = ((), (), s32[]{:S(2)}) async-start(), calls=%async_computation.23 | async-start | bytes 1889280 | tf_op jit(solution)/shard_map/all_gather | solution.py:97
  12.4 264.9 %reduce-scatter.24.cloned.1.call-start = ((), (), s32[]{:S(2)}) async-start(), calls=%async_computation.11 | async-start | bytes 1966080 | tf_op jit(solution)/shard_map/reduce_scatter | solution.py:120
  13.1 79.1 %copy-start.112 = (pred[2]{0:T(512)(128)(4,1)}, pred[2]{0:T(512)(128)(4,1)S(1)}, u32[]{:S(2)}) copy-start(pred[2]{0:T(512)(128)(4,1)S(1)} %get-tuple-element.85) | copy-start | bytes 10
  90.5 336.0 %copy-start.67 = (f32[3,64]{1,0:T(4,128)}, f32[3,64]{1,0:T(4,128)S(1)}, u32[]{:S(2)}) copy-start(f32[3,64]{1,0:T(4,128)S(1)} %get-tuple-element.140) | copy-start | bytes 2308
  99.0 176.4 %copy-start.41 = (bf16[2,3,64,512]{3,2,1,0:T(8,128)(2,1)}, bf16[2,3,64,512]{3,2,1,0:T(8,128)(2,1)S(1)}, u32[]{:S(2)}) copy-start(bf16[2,3,64,512]{3,2,1,0:T(8,128)(2,1)S(1)} %fusion.90) | copy-start | bytes 1179652
  99.0 43.2 %copy-start.119 = (bf16[2,24]{1,0:T(2,128)(2,1)S(1)}, bf16[2,24]{1,0:T(2,128)(2,1)}, u32[]{:S(2)}) copy-start(bf16[2,24]{1,0:T(2,128)(2,1)} %param.25) | copy-start | bytes 292
  99.0 108.8 %copy-start.118 = (bf16[4,24]{1,0:T(4,128)(2,1)S(1)}, bf16[4,24]{1,0:T(4,128)(2,1)}, u32[]{:S(2)}) copy-start(bf16[4,24]{1,0:T(4,128)(2,1)} %param.26) | copy-start | bytes 580
  100.8 174.6 %copy-start.63 = (bf16[2,10,768]{2,1,0:T(8,128)(2,1)S(1)}, bf16[2,10,768]{2,1,0:T(8,128)(2,1)}, u32[]{:S(2)}) copy-start(bf16[2,10,768]{2,1,0:T(8,128)(2,1)} %copy-done.62) | copy-start | bytes 92164
  100.8 179.2 %all-gather.12.cloned.1.call-start = ((), (), s32[]{:S(2)}) async-start(), calls=%async_computation.12 | async-start | bytes 4866048 | tf_op jit(solution)/shard_map/all_gather | solution.py:75
  101.4 184.6 %all-gather.14.cloned.1.call-start = ((), (), s32[]{:S(2)}) async-start(), calls=%async_computation.13 | async-start | bytes 4866048 | tf_op jit(solution)/shard_map/all_gather | solution.py:76
  102.0 253.5 %reduce-scatter.26.cloned.1.call-start = ((), (), s32[]{:S(2)}) async-start(), calls=%async_computation.14 | async-start | bytes 1966080 | tf_op jit(solution)/shard_map/reduce_scatter | solution.py:120
  142.2 137.9 %copy-start.96 = (f32[3072]{0:T(1024)}, f32[3072]{0:T(1024)S(1)}, u32[]{:S(2)}) copy-start(f32[3072]{0:T(1024)S(1)} %convert_element_type.307) | copy-start | bytes 36868
  272.7 7.4 copy-start.71
  272.7 182.3 %copy-start.59 = (f32[768]{0:T(1024)}, f32[768]{0:T(1024)S(1)}, u32[]{:S(2)}) copy-start(f32[768]{0:T(1024)S(1)} %get-tuple-element.143) | copy-start | bytes 9220
  278.7 7.3 copy-start.89
  286.1 24.4 %copy-start.58 = (bf16[768,10]{0,1:T(8,128)(2,1)S(1)}, bf16[768,10]{0,1:T(8,128)(2,1)}, u32[]{:S(2)}) copy-start(bf16[768,10]{0,1:T(8,128)(2,1)} %copy-done.57) | copy-start | bytes 46084
  286.1 24.4 %copy-start.114 = (pred[2]{0:T(512)(128)(4,1)S(1)}, pred[2]{0:T(512)(128)(4,1)}, u32[]{:S(2)}) copy-start(pred[2]{0:T(512)(128)(4,1)} %get-tuple-element.84) | copy-start | bytes 10
  291.6 21.5 %copy-start.83 = (f32[2,128]{1,0:T(2,128)}, f32[2,128]{1,0:T(2,128)S(1)}, u32[]{:S(2)}) copy-start(f32[2,128]{1,0:T(2,128)S(1)} %broadcast_multiply_fusion.2) | copy-start | bytes 3076
  291.8 21.3 %copy-start.103 = (f32[2,128]{1,0:T(2,128)}, f32[2,128]{1,0:T(2,128)S(1)}, u32[]{:S(2)}) copy-start(f32[2,128]{1,0:T(2,128)S(1)} %multiply_reduce_fusion.10) | copy-start | bytes 3076
  291.8 21.3 %copy-start.87 = (f32[2,128]{1,0:T(2,128)}, f32[2,128]{1,0:T(2,128)S(1)}, u32[]{:S(2)}) copy-start(f32[2,128]{1,0:T(2,128)S(1)} %fusion.132) | copy-start | bytes 3076
  310.5 12.0 %copy-start.65 = (bf16[2,10,768]{2,1,0:T(8,128)(2,1)}, bf16[2,10,768]{2,1,0:T(8,128)(2,1)S(1)}, u32[]{:S(2)}) copy-start(bf16[2,10,768]{2,1,0:T(8,128)(2,1)S(1)} %broadcast_select_fusion) | copy-start | bytes 92164
  322.2 36.2 %copy-start.72 = (f32[768]{0:T(1024)S(1)}, f32[768]{0:T(1024)}, u32[]{:S(2)}) copy-start(f32[768]{0:T(1024)} %copy-done.71) | copy-start | bytes 9220
  322.2 36.2 %copy-start.97 = (f32[3072]{0:T(1024)S(1)}, f32[3072]{0:T(1024)}, u32[]{:S(2)}) copy-start(f32[3072]{0:T(1024)} %copy-done.96) | copy-start | bytes 36868
  322.2 91.1 %all-gather.16.cloned.1.call-start = ((), (), s32[]{:S(2)}) async-start(), calls=%async_computation.15 | async-start | bytes 1966080 | tf_op jit(solution)/shard_map/all_gather | solution.py:191
  355.5 7.2 slice-start.8
  357.0 17.3 %copy-start.94 = (f32[2,128]{1,0:T(2,128)}, f32[2,128]{1,0:T(2,128)S(1)}, u32[]{:S(2)}) copy-start(f32[2,128]{1,0:T(2,128)S(1)} %broadcast_multiply_fusion.1) | copy-start | bytes 3076
  358.4 15.8 %copy-start.108 = (f32[2,128]{1,0:T(2,128)}, f32[2,128]{1,0:T(2,128)S(1)}, u32[]{:S(2)}) copy-start(f32[2,128]{1,0:T(2,128)S(1)} %fusion.133) | copy-start | bytes 3076
  377.1 140.8 %all-gather.18.cloned.1.call-start = ((), (), s32[]{:S(2)}) async-start(), calls=%async_computation.16 | async-start | bytes 1966080 | tf_op jit(solution)/shard_map/all_gather | solution.py:191
  415.5 9.2 slice-start.2
  428.3 24.3 %copy-start.84 = (f32[2,128]{1,0:T(2,128)S(1)}, f32[2,128]{1,0:T(2,128)}, u32[]{:S(2)}) copy-start(f32[2,128]{1,0:T(2,128)} %copy-done.83) | copy-start | bytes 3076
  429.9 22.8 %copy-start.21 = (bf16[2,2,128,768]{3,2,1,0:T(8,128)(2,1)S(1)}, bf16[2,2,128,768]{3,2,1,0:T(8,128)(2,1)}, u32[]{:S(2)}) copy-start(bf16[2,2,128,768]{3,2,1,0:T(8,128)(2,1)} %param.27) | copy-start | bytes 2359300
  452.6 9.7 slice-start.6
  456.4 6.0 copy-start.100
  456.4 6.0 copy-start.10
  456.4 6.0 copy-start.12
  456.4 6.0 copy-start.90
  467.4 124.1 %reduce-scatter.34.cloned.1.call-start = ((), (), s32[]{:S(2)}) async-start(), calls=%async_computation.20 | async-start | bytes 5898240 | tf_op jit(solution)/shard_map/reduce_scatter | solution.py:285
  476.9 202.5 %reduce-scatter.30.cloned.1.call-start = ((), (), s32[]{:S(2)}) async-start(), calls=%async_computation.18 | async-start | bytes 5898240 | tf_op jit(solution)/shard_map/reduce_scatter | solution.py:282
  497.5 204.2 %reduce-scatter.42.cloned.1.call-start = ((), (), s32[]{:S(2)}) async-start(), calls=%async_computation.26 | async-start | bytes 245760
  513.1 208.4 %reduce-scatter.44.cloned.1.call-start = ((), (), s32[]{:S(2)}) async-start(), calls=%async_computation.27 | async-start | bytes 245760
  515.6 225.7 %reduce-scatter.38.cloned.1.call-start = ((), (), s32[]{:S(2)}) async-start(), calls=%async_computation.24 | async-start | bytes 245760
  520.1 8.6 slice-start
  524.1 8.2 copy-start.39
  532.4 24.6 %copy-start.113 = (pred[2]{0:T(512)(128)(4,1)S(1)}, pred[2]{0:T(512)(128)(4,1)}, u32[]{:S(2)}) copy-start(pred[2]{0:T(512)(128)(4,1)} %copy-done.112) | copy-start | bytes 10
  532.4 24.7 %copy-start.61 = (f32[10,768]{1,0:T(8,128)S(1)}, f32[10,768]{1,0:T(8,128)}, u32[]{:S(2)}) copy-start(f32[10,768]{1,0:T(8,128)} %get-tuple-element.118) | copy-start | bytes 92164
  533.9 24.4 %copy-start.42 = (bf16[2,3,64,512]{3,2,1,0:T(8,128)(2,1)S(1)}, bf16[2,3,64,512]{3,2,1,0:T(8,128)(2,1)}, u32[]{:S(2)}) copy-start(bf16[2,3,64,512]{3,2,1,0:T(8,128)(2,1)} %copy-done.41) | copy-start | bytes 1179652
  558.3 219.6 %reduce-scatter.40.cloned.1.call-start = ((), (), s32[]{:S(2)}) async-start(), calls=%async_computation.25 | async-start | bytes 884736
  561.4 336.6 %all-reduce.16.cloned.1.call-start = ((), (), s32[]{:S(2)}) async-start(), calls=%async_computation.28 | async-start | bytes 6045696
  570.4 372.9 %reduce-scatter.28.cloned.1.call-start = ((), (), s32[]{:S(2)}) async-start(), calls=%async_computation.17 | async-start | bytes 2654208 | tf_op jit(solution)/shard_map/reduce_scatter | solution.py:311
  576.6 413.5 %reduce-scatter.36.cloned.1.call-start = ((), (), s32[]{:S(2)}) async-start(), calls=%async_computation.21 | async-start | bytes 2654208 | tf_op jit(solution)/shard_map/reduce_scatter | solution.py:303
  594.4 88.0 %copy-start.122 = (u32[32]{0:T(128)S(1)}, u32[32]{0:T(128)}, u32[]{:S(2)}) copy-start(u32[32]{0:T(128)} %constant.96) | copy-start | bytes 388
  594.4 90.6 %copy-start.121 = (u32[32]{0:T(128)S(1)}, u32[32]{0:T(128)}, u32[]{:S(2)}) copy-start(u32[32]{0:T(128)} %constant.88) | copy-start | bytes 388
  594.4 92.4 %copy-start.60 = (f32[768]{0:T(1024)S(1)}, f32[768]{0:T(1024)}, u32[]{:S(2)}) copy-start(f32[768]{0:T(1024)} %copy-done.59) | copy-start | bytes 9220
  594.4 92.4 %copy-start.76 = (f32[768]{0:T(1024)S(1)}, f32[768]{0:T(1024)}, u32[]{:S(2)}) copy-start(f32[768]{0:T(1024)} %get-tuple-element.77) | copy-start | bytes 9220
  594.4 92.4 %copy-start.85 = (f32[2,128]{1,0:T(2,128)S(1)}, f32[2,128]{1,0:T(2,128)}, u32[]{:S(2)}) copy-start(f32[2,128]{1,0:T(2,128)} %copy-done.83) | copy-start | bytes 3076
  594.4 92.4 %copy-start.88 = (f32[2,128]{1,0:T(2,128)S(1)}, f32[2,128]{1,0:T(2,128)}, u32[]{:S(2)}) copy-start(f32[2,128]{1,0:T(2,128)} %copy-done.87) | copy-start | bytes 3076
  594.4 92.6 %copy-start.35 = (bf16[2,1,128,768]{3,2,0,1:T(8,128)(2,1)S(1)}, bf16[2,1,128,768]{3,2,0,1:T(8,128)(2,1)}, u32[]{:S(2)}) copy-start(bf16[2,1,128,768]{3,2,0,1:T(8,128)(2,1)} %get-tuple-element.111) | copy-start | bytes 1179652
  594.4 441.9 %reduce-scatter.32.cloned.1.call-start = ((), (), s32[]{:S(2)}) async-start(), calls=%async_computation.19 | async-start | bytes 2654208 | tf_op jit(solution)/shard_map/reduce_scatter | solution.py:302
  682.4 40.0 %copy-start.40 = (bf16[2,3,64,512]{3,2,1,0:T(8,128)(2,1)S(1)}, bf16[2,3,64,512]{3,2,1,0:T(8,128)(2,1)}, u32[]{:S(2)}) copy-start(bf16[2,3,64,512]{3,2,1,0:T(8,128)(2,1)} %copy-done.39) | copy-start | bytes 1179652
  687.2 35.4 %copy-start.49 = (bf16[2,3,64,512]{3,2,1,0:T(8,128)(2,1)S(1)}, bf16[2,3,64,512]{3,2,1,0:T(8,128)(2,1)}, u32[]{:S(2)}) copy-start(bf16[2,3,64,512]{3,2,1,0:T(8,128)(2,1)} %copy-done.48) | copy-start | bytes 1179652
  (87 other events, 283.2 us)
Sparse Core Ops, SparseCore 0:
  11.3 39.8 all-gather.19
  52.8 35.8 all-gather.21
  101.0 32.4 reduce-scatter.23
  136.1 62.6 all-gather.11
  201.4 62.4 all-gather.13
  322.3 33.1 reduce-scatter.25
  377.2 36.0 all-gather.15
  467.5 35.3 all-gather.17
  505.2 86.2 reduce-scatter.33
  593.6 85.7 reduce-scatter.29
  681.7 19.8 reduce-scatter.41
  703.9 17.5 reduce-scatter.43
  723.7 17.5 reduce-scatter.37
  744.6 33.1 reduce-scatter.39
  780.3 117.6 all-reduce.15
  901.8 41.4 reduce-scatter.27
  947.5 42.4 reduce-scatter.35
  993.8 42.4 reduce-scatter.31
where the time goes:
time: 1050 us; the launch traced here: 1040 us
  waiting for transfers between devices  478 us (46%)
  blocking collectives  323 us (31%)
  matrix products  98.1 us (9%)
  local copies, waits for them, and re-layouts  75 us (7%)
  other arithmetic  47.8 us (5%)
  between operations  20.2 us (2%)
    unnamed x23, waiting for transfers between devices  180 us
    reduce_scatter x1, waiting for transfers between devices, local(): lax.psum_scatter(ffn_total[0].astype(jnp.bfloat16), 'head', scatter_dimen...  85 us
    all_gather x1, blocking collectives, local(): lax.all_gather(init_memory, ('dp', 'head'), axis=1, tiled=True)  73 us
    all_gather x1, blocking collectives, local(): lax.all_gather(norm_gains, ('dp', 'head'), axis=1, tiled=True)  65.3 us
    all_gather x1, blocking collectives, local(): lax.all_gather(biases, ('dp', 'head'), axis=1, tiled=True)  64 us
    unnamed x2, blocking collectives  62.3 us
    reduce_scatter x1, waiting for transfers between devices, local(): lax.psum_scatter(partial_sums[1], 'dp', scatter_dimension=0, tiled=True)  46.7 us
    reduce_scatter x1, waiting for transfers between devices, local(): lax.psum_scatter(partial_sums[0], 'dp', scatter_dimension=1, tiled=True)  46.3 us
  transfers between devices with their start and end apart: 18, of which 12 were waited for; matrix products, arithmetic and copies ran while one was open for 13% of the time, Pallas kernels for 0%

commit v1 on v0

--- a/solution.py
+++ b/solution.py
@@ -1,9 +1,52 @@
+import functools
+
 import jax
 import jax.numpy as jnp
 from jax import lax
+from jax.experimental import pallas as pl
+from jax.experimental.pallas import tpu as pltpu
 from jax.sharding import PartitionSpec as P
 
 HD = 64
+MESH = pl.DeviceIdType.MESH
+BF = jnp.bfloat16
+F32 = jnp.float32
+VMEM_LIMIT = 64 * 1024 * 1024
+
+
+def nn(a, b):
+    return lax.dot_general(a, b, (((1,), (0,)), ((), ())), preferred_element_type=F32)
+
+
+def nt(a, b):
+    return lax.dot_general(a, b, (((1,), (1,)), ((), ())), preferred_element_type=F32)
+
+
+def tn(a, b):
+    return lax.dot_general(a, b, (((0,), (0,)), ((), ())), preferred_element_type=F32)
+
+
+def place():
+    dp, z = lax.axis_index("dp"), lax.axis_index("head")
+    core, plane = dp % 2, dp // 2
+    return core, plane % 2, plane // 2, z
+
+
+def device(core, x, y, z):
+    return ((y * 2 + x) * 2 + core, z)
+
+
+def push(src, dst, send, recv, target):
+    return pltpu.make_async_remote_copy(
+        src_ref=src, dst_ref=dst, send_sem=send, recv_sem=recv, device_id=target, device_id_type=MESH
+    )
+
+
+def greet(targets):
+    barrier = pltpu.get_barrier_semaphore()
+    for target in targets:
+        pl.semaphore_signal(barrier, inc=1, device_id=target, device_id_type=MESH)
+    pl.semaphore_wait(barrier, len(targets))
 
 
 def from_root(x, axis, root):
@@ -329,9 +372,990 @@
     )
 
 
+def layer_kernel(
+    mem_rows,
+    rows_ref, wa, wf, lab_row, lab_col, par, bqv, bin_ref, mem_a, mem_b, init_a, init_b, flags,
+    y_out, dt_out, ffg_out, agq_out, ago_out, sg_out, dinit_out, dbin_out, dbqv_out,
+    x, qkv, pt, ot, mask, hf, acc, xh1, rs1, hb, u, gp, xh2, rs2, gf, gz, ga, got, gq,
+    send_buf, recv_buf, cur_a, cur_b, carry, stage, send_sem, recv_sem, stage_sem,
+):
+    core, px, py, z = place()
+    sibling = device(1 - core, px, py, z)
+    greet([sibling])
+    seg_len, width = x.shape[1], x.shape[2]
+    hidden = u.shape[2]
+    heads = pt.shape[1]
+    local = ot.shape[2]
+    per_block = local // HD
+    step = 128
+    row_steps = seg_len // step
+    hid = 256
+    hid_steps = hidden // hid
+    text_rows = (seg_len - 2 * mem_rows) // row_steps
+    tail = 16
+
+    def rows(r):
+        return pl.ds(pl.multiple_of(r * step, step), step)
+
+    def cols(i):
+        return pl.ds(pl.multiple_of(i * hid, hid), hid)
+
+    def head_rows(h, part):
+        return pl.ds(pl.multiple_of((h % per_block) * HD + part * local, HD), HD)
+
+    def exchange(slot, r):
+        return push(
+            send_buf.at[slot, r], recv_buf.at[slot, r], send_sem.at[slot, r], recv_sem.at[slot, r], sibling
+        )
+
+    def place_rows(start, count):
+        nat = lax.broadcasted_iota(jnp.int32, (count, seg_len), 0) + start
+        pad = lax.broadcasted_iota(jnp.int32, (count, seg_len), 1)
+        inside = pad & (step - 1)
+        target = (pad >> 7) * text_rows + inside + mem_rows
+        return jnp.where((nat == target) & (inside < text_rows), 1.0, 0.0).astype(BF)
+
+    def take_rows(r):
+        inside = lax.broadcasted_iota(jnp.int32, (step, seg_len), 0)
+        nat = lax.broadcasted_iota(jnp.int32, (step, seg_len), 1)
+        target = r * text_rows + inside + mem_rows
+        return jnp.where((nat == target) & (inside < text_rows), 1.0, 0.0).astype(BF)
+
+    def loop(count, body):
+        def run(i, unused):
+            body(i)
+            return unused
+
+        lax.fori_loop(0, count, run, 0)
+
+    sg_out[...] = jnp.zeros_like(sg_out)
+    dinit_out[...] = jnp.zeros_like(dinit_out)
+    dbin_out[...] = jnp.zeros_like(dbin_out)
+    dbqv_out[...] = jnp.zeros_like(dbqv_out)
+    carry[...] = jnp.zeros_like(carry)
+    cur_a[...] = mem_a[...]
+    cur_b[...] = mem_b[...]
+    tail_row = lax.broadcasted_iota(jnp.int32, (tail, width), 0)
+    is_mem = tail_row >= tail - mem_rows
+
+    def forward(seg):
+        def build(r):
+            x[seg, rows(r), :] = nn(place_rows(r * step, step), rows_ref[seg]).astype(BF)
+
+        loop(row_steps, build)
+        x[seg, 0:tail, :] = x[seg, 0:tail, :] + cur_a[...]
+        x[seg, seg_len - tail : seg_len, :] = x[seg, seg_len - tail : seg_len, :] + cur_b[...]
+        left, right = lab_col[seg], lab_row[seg]
+        mask[...] = jnp.where((left == right) | (left < 0) | (right < 0), 0.0, -1e30)
+
+        def project(i):
+            j, t = i // 3, i % 3
+            at = pl.ds(pl.multiple_of(t * local, local), local)
+            value = nt(wa[j, at, :], x[seg]) + bqv[j, at, :]
+            qkv[seg, j, at, :] = (value * jnp.where(t == 0, 0.125, 1.0)).astype(BF)
+
+        loop(6, project)
+
+        def attend(h):
+            j = h // per_block
+            q, k, v = (qkv[seg, j, head_rows(h, part), :] for part in range(3))
+            s = tn(k, q) + mask[...]
+            e = jnp.exp(s - jnp.max(s, axis=0, keepdims=True))
+            p = (e * (1.0 / jnp.sum(e, axis=0, keepdims=True))).astype(BF)
+            pt[seg, h] = p
+            ot[seg, j, head_rows(h, 0), :] = nn(v, p).astype(BF)
+
+        loop(heads, attend)
+
+        def out_proj(r):
+            part = tn(ot[seg, 0, :, rows(r)], wa[0, 3 * local :, :]) + tn(
+                ot[seg, 1, :, rows(r)], wa[1, 3 * local :, :]
+            )
+            acc[rows(r), :] = part
+            send_buf[0, r] = part.astype(BF)
+            exchange(0, r).start()
+
+        loop(row_steps, out_proj)
+
+        def norm(v):
+            center = v - jnp.mean(v, axis=-1, keepdims=True)
+            scale = lax.rsqrt(jnp.mean(center * center, axis=-1, keepdims=True) + 1e-05)
+            return center * scale, scale
+
+        def norm_one(r):
+            exchange(0, r).wait()
+            h0 = (
+                x[seg, rows(r), :].astype(F32)
+                + acc[rows(r), :]
+                + recv_buf[0, r].astype(F32)
+                + par[3:4, :]
+            )
+            hat, scale = norm(h0)
+            xh1[seg, rows(r), :] = hat.astype(BF)
+            rs1[seg, rows(r), :] = scale
+            h = hat * par[0:1, :] + par[2:3, :]
+            hf[rows(r), :] = h
+            hb[seg, rows(r), :] = h.astype(BF)
+
+        loop(row_steps, norm_one)
+
+        def inner(i):
+            v = nt(hb[seg], wf[0, cols(i), :]) + bin_ref[:, cols(i)]
+            c0 = 0.7978845608028654
+            sq = v * v
+            th = jnp.tanh(v * (c0 + (c0 * 0.044715) * sq))
+            half = 0.5 + 0.5 * th
+            u[seg, :, cols(i)] = (v * half).astype(BF)
+            slope = half + (0.5 * v) * (1.0 - th * th) * (c0 + (3 * c0 * 0.044715) * sq)
+            gp[seg, :, cols(i)] = slope.astype(BF)
+
+        loop(hid_steps, inner)
+
+        def outer(r):
+            part = nn(u[seg, rows(r), :], wf[1])
+            acc[rows(r), :] = part
+            send_buf[1, r] = part.astype(BF)
+            exchange(1, r).start()
+
+        loop(row_steps, outer)
+
+        def norm_two(r):
+            exchange(1, r).wait()
+            post = hf[rows(r), :] + acc[rows(r), :] + recv_buf[1, r].astype(F32) + par[4:5, :]
+            hat, scale = norm(post)
+            xh2[seg, rows(r), :] = hat.astype(BF)
+            rs2[seg, rows(r), :] = scale
+            y_out[seg, rows(r), :] = (hat * par[1:2, :] + par[5:6, :]).astype(BF)
+
+        loop(row_steps, norm_two)
+        last = y_out[seg, seg_len - tail : seg_len, :].astype(F32)
+        chosen = jnp.where(flags[1:2, :] > 0, init_b[...].astype(F32), last)
+        memory = jnp.where(is_mem, chosen, 0.0)
+        cur_b[...] = memory.astype(BF)
+        cur_a[...] = pltpu.roll(memory, mem_rows, 0).astype(BF)
+
+    def backward(seg):
+        def pull_two(r):
+            g_y = rows_ref[2 + seg, rows(r), :].astype(F32) + jnp.where(r == row_steps - 1, carry[...], 0.0)
+            hat = xh2[seg, rows(r), :].astype(F32)
+            g = g_y * par[1:2, :]
+            m1 = jnp.mean(g, axis=-1, keepdims=True)
+            m2 = jnp.mean(g * hat, axis=-1, keepdims=True)
+            pre = rs2[seg, rows(r), :] * (g - m1 - hat * m2)
+            hf[rows(r), :] = pre
+            gf[seg, rows(r), :] = pre.astype(BF)
+            sg_out[1:2, :] += jnp.sum(g_y * hat, axis=0, keepdims=True)
+            sg_out[5:6, :] += jnp.sum(g_y, axis=0, keepdims=True)
+            sg_out[4:5, :] += jnp.sum(pre, axis=0, keepdims=True)
+
+        loop(row_steps, pull_two)
+
+        def pull_inner(i):
+            g_u = nt(gf[seg], wf[1, cols(i), :])
+            g_z = (g_u * gp[seg, :, cols(i)].astype(F32)).astype(BF)
+            gz[seg, :, cols(i)] = g_z
+            dbin_out[0:1, cols(i)] += jnp.sum(g_z.astype(F32), axis=0, keepdims=True)
+
+        loop(hid_steps, pull_inner)
+
+        def pull_hidden(r):
+            part = nn(gz[seg, rows(r), :], wf[0])
+            acc[rows(r), :] = part
+            send_buf[0, r] = part.astype(BF)
+            exchange(0, r).start()
+
+        loop(row_steps, pull_hidden)
+
+        def pull_one(r):
+            exchange(0, r).wait()
+            g_h = hf[rows(r), :] + acc[rows(r), :] + recv_buf[0, r].astype(F32)
+            hat = xh1[seg, rows(r), :].astype(F32)
+            g = g_h * par[0:1, :]
+            m1 = jnp.mean(g, axis=-1, keepdims=True)
+            m2 = jnp.mean(g * hat, axis=-1, keepdims=True)
+            pre = rs1[seg, rows(r), :] * (g - m1 - hat * m2)
+            hf[rows(r), :] = pre
+            ga[seg, rows(r), :] = pre.astype(BF)
+            sg_out[0:1, :] += jnp.sum(g_h * hat, axis=0, keepdims=True)
+            sg_out[2:3, :] += jnp.sum(g_h, axis=0, keepdims=True)
+            sg_out[3:4, :] += jnp.sum(pre, axis=0, keepdims=True)
+
+        loop(row_steps, pull_one)
+
+        def pull_out(j):
+            got[j] = nt(wa[j, 3 * local :, :], ga[seg]).astype(BF)
+
+        loop(2, pull_out)
+
+        def pull_head(h):
+            j = h // per_block
+            q, k, v = (qkv[seg, j, head_rows(h, part), :] for part in range(3))
+            g_o = got[j, head_rows(h, 0), :]
+            p = pt[seg, h]
+            d_v = nt(g_o, p).astype(BF)
+            total = jnp.sum(
+                g_o.astype(F32) * ot[seg, j, head_rows(h, 0), :].astype(F32), axis=0, keepdims=True
+            )
+            d_s = (p.astype(F32) * (tn(v, g_o) - total)).astype(BF)
+            d_q = (nn(k, d_s) * 0.125).astype(BF)
+            d_k = nt(q, d_s).astype(BF)
+            for part, value in enumerate((d_q, d_k, d_v)):
+                gq[seg, j, head_rows(h, part), :] = value
+            for part, value in ((0, d_q), (2, d_v)):
+                dbqv_out[j, head_rows(h, part), :] += jnp.sum(value.astype(F32), axis=1, keepdims=True)
+
+        loop(heads, pull_head)
+
+        def pull_rows(r):
+            part = tn(gq[seg, 0, :, rows(r)], wa[0, : 3 * local, :]) + tn(
+                gq[seg, 1, :, rows(r)], wa[1, : 3 * local, :]
+            )
+            acc[rows(r), :] = part
+            send_buf[1, r] = part.astype(BF)
+            exchange(1, r).start()
+
+        loop(row_steps, pull_rows)
+
+        def pull_x(r):
+            exchange(1, r).wait()
+            total = hf[rows(r), :] + acc[rows(r), :] + recv_buf[1, r].astype(F32)
+            acc[rows(r), :] = total
+            xh1[seg, rows(r), :] = total.astype(BF)
+
+        loop(row_steps, pull_x)
+
+        def out_text(r):
+            dt_out[seg, rows(r), :] = nn(take_rows(r), xh1[seg]).astype(BF)
+
+        loop(row_steps, out_text)
+        both = pltpu.roll(acc[0:tail, :], tail - mem_rows, 0) + acc[seg_len - tail : seg_len, :]
+        memory = jnp.where(is_mem, both, 0.0)
+        flag = jnp.where(seg == 0, flags[0:1, :], flags[1:2, :])
+        dinit_out[...] += jnp.where(flag > 0, memory, 0.0)
+        carry[step - tail : step, :] = jnp.where(flag > 0, 0.0, memory)
+
+    loop(2, forward)
+    loop(2, lambda i: backward(1 - i))
+
+    def stored(kind, i):
+        return pltpu.make_async_copy(stage.at[kind], ffg_out.at[kind, cols(i), :], stage_sem.at[kind])
+
+    def ffn_grads(i):
+        for kind, (left, right) in enumerate(((gz, hb), (u, gf))):
+            value = tn(left[0, :, cols(i)], right[0]) + tn(left[1, :, cols(i)], right[1])
+
+            @pl.when(i > 0)
+            def _():
+                stored(kind, i - 1).wait()
+
+            stage[kind] = value.astype(BF)
+            stored(kind, i).start()
+
+    loop(hid_steps, ffn_grads)
+    for kind in range(2):
+        stored(kind, hid_steps - 1).wait()
+
+    def attention_grads(i):
+        xt = [x[s, :, cols(i)].T for s in range(2)]
+        gt = [ga[s, :, cols(i)].T for s in range(2)]
+        for j in range(2):
+            agq_out[j, cols(i), :] = (nt(xt[0], gq[0, j]) + nt(xt[1], gq[1, j])).astype(BF)
+            ago_out[j, cols(i), :] = (nt(gt[0], ot[0, j]) + nt(gt[1], ot[1, j])).astype(BF)
+
+    loop(width // hid, attention_grads)
+
+
+def start_kernel(
+    dp_count, head_count,
+    small, seqf, memp, rows, wa, wf,
+    small_o, seqf_o, memp_o, rows_o, wa_o, wf_o,
+    small_s, small_r, pair_s, pair_r, rows_s, rows_r, fwd_s, fwd_r, att_s, att_r, plane_s, plane_r,
+    ffn_s, ffn_r, side_s, side_r, local_sem,
+):
+    core, px, py, z = place()
+    plane = py * 2 + px
+    me = (plane * 2 + core) * head_count + z
+    total = dp_count * head_count
+    sibling = device(1 - core, px, py, z)
+    x_mate, y_mate = device(core, 1 - px, py, z), device(core, px, 1 - py, z)
+    x_plane, y_plane, far_plane = py * 2 + 1 - px, (1 - py) * 2 + px, (1 - py) * 2 + 1 - px
+
+    def other(i):
+        t = (me + 1 + i) % total
+        return t, (t // head_count, t % head_count)
+
+    def loop(count, body):
+        def run(i, unused):
+            body(i)
+            return unused
+
+        lax.fori_loop(0, count, run, 0)
+
+    barrier = pltpu.get_barrier_semaphore()
+    loop(
+        total - 1,
+        lambda i: pl.semaphore_signal(barrier, inc=1, device_id=other(i)[1], device_id_type=MESH),
+    )
+    pl.semaphore_wait(barrier, total - 1)
+
+    locals_ = [
+        pltpu.make_async_copy(small, small_o.at[me], local_sem.at[0]),
+        pltpu.make_async_copy(wf, wf_o.at[:, plane * head_count + z], local_sem.at[1]),
+    ]
+    for copy in locals_:
+        copy.start()
+    own_attention = pltpu.make_async_copy(wa, wa_o.at[z % 2], local_sem.at[2])
+    is_home = core == z // 2
+
+    @pl.when(is_home)
+    def _():
+        own_attention.start()
+
+    share = wa.shape[0] // 4
+    half = share // 2
+    mine = pl.ds(share * plane + half * core, half)
+
+    def attention_out(i):
+        zt = (z + 1 + i) % head_count
+        return push(
+            wa.at[mine],
+            wa_o.at[z % 2, mine],
+            att_s.at[i],
+            att_r.at[z % 2, core],
+            device(z // 2, px, py, zt),
+        )
+
+    for i in range(head_count - 1):
+        attention_out(i).start()
+
+    piece = rows.shape[2] // 2
+
+    def rows_out(j, h):
+        span = pl.ds(h * piece, piece)
+        return push(
+            rows.at[j, :, span],
+            rows_o.at[:, z, span],
+            rows_s.at[j, h],
+            rows_r.at[z],
+            device(h, px, py, 2 * core + j),
+        )
+
+    def rows_here(j, h):
+        span = pl.ds(h * piece, piece)
+        return pltpu.make_async_copy(rows.at[j, :, span], rows_o.at[:, z, span], local_sem.at[3])
+
+    for j in range(2):
+        for h in range(2):
+            here = (core == h) & (z == 2 * core + j)
+
+            @pl.when(here)
+            def _():
+                rows_here(j, h).start()
+
+            @pl.when(jnp.logical_not(here))
+            def _():
+                rows_out(j, h).start()
+
+    def ffn_out(i):
+        zt = (z + 1 + i) % head_count
+        return push(
+            wf,
+            wf_o.at[:, plane * head_count + z],
+            ffn_s.at[i],
+            ffn_r.at[z],
+            device(core, px, py, zt),
+        )
+
+    for i in range(head_count - 1):
+        ffn_out(i).start()
+
+    pair = [
+        push(seqf, seqf_o, pair_s.at[0], pair_r.at[0], sibling),
+        push(memp, memp_o, pair_s.at[1], pair_r.at[1], sibling),
+    ]
+    for copy in pair:
+        copy.start()
+
+    def small_out(i):
+        return push(small, small_o.at[me], small_s.at[i], small_r.at[me], other(i)[1])
+
+    loop(total - 1, lambda i: small_out(i).start())
+
+    def plane_copy(k, which):
+        block = pl.ds(share * plane, share)
+        if which == 0:
+            return push(wa_o.at[k, block], wa_o.at[k, block], plane_s.at[k, 0], plane_r.at[k, 0], x_mate)
+        if which == 1:
+            return push(wa_o.at[k, block], wa_o.at[k, block], plane_s.at[k, 1], plane_r.at[k, 1], y_mate)
+        if which == 2:
+            block = pl.ds(share * x_plane, half)
+            return push(wa_o.at[k, block], wa_o.at[k, block], plane_s.at[k, 2], plane_r.at[k, 2], y_mate)
+        block = pl.ds(share * y_plane + half, half)
+        return push(wa_o.at[k, block], wa_o.at[k, block], plane_s.at[k, 3], plane_r.at[k, 3], x_mate)
+
+    foreign = [jnp.logical_not(is_home & (z % 2 == k)) for k in range(2)]
+
+    def arrived(k, h):
+        span = pl.ds(share * plane + half * h, half)
+        return push(wa.at[mine], wa_o.at[k, span], att_s.at[0], att_r.at[k, h], sibling)
+
+    for k in range(2):
+
+        @pl.when(foreign[k])
+        def _():
+            for h in range(2):
+                arrived(k, h).wait_recv()
+            plane_copy(k, 0).start()
+            plane_copy(k, 1).start()
+
+    def forward(zs):
+        span = pl.ds(core * piece, piece)
+        return push(
+            rows_o.at[:, zs, span], rows_o.at[:, zs, span], fwd_s.at[zs], fwd_r.at[zs], sibling
+        )
+
+    def rows_arrived(zs):
+        span = pl.ds(core * piece, piece)
+        return push(rows.at[0, :, span], rows_o.at[:, zs, span], rows_s.at[0, 0], rows_r.at[zs], sibling)
+
+    for zs in range(head_count):
+        here = is_home & (z == zs)
+
+        @pl.when(here)
+        def _():
+            rows_here(z % 2, core).wait()
+
+        @pl.when(jnp.logical_not(here))
+        def _():
+            rows_arrived(zs).wait_recv()
+
+        forward(zs).start()
+
+    def side(kind, zi, first):
+        own, x_at, y_at = (p * head_count + zi for p in (plane, x_plane, y_plane))
+        if first == 0:
+            return push(wf_o.at[kind, own], wf_o.at[kind, own], side_s.at[zi, kind, 0], side_r.at[zi, kind, 0], x_mate)
+        if first == 1:
+            return push(wf_o.at[kind, own], wf_o.at[kind, own], side_s.at[zi, kind, 1], side_r.at[zi, kind, 1], y_mate)
+        if kind == 0:
+            return push(wf_o.at[0, x_at], wf_o.at[0, x_at], side_s.at[zi, 0, 2], side_r.at[zi, 0, 2], y_mate)
+        return push(wf_o.at[1, y_at], wf_o.at[1, y_at], side_s.at[zi, 1, 2], side_r.at[zi, 1, 2], x_mate)
+
+    def ffn_arrived(zs):
+        return push(wf, wf_o.at[:, plane * head_count + zs], ffn_s.at[0], ffn_r.at[zs], sibling)
+
+    for d in range(head_count):
+        zi = (z + d) % head_count
+        if d == 0:
+            locals_[1].wait()
+        else:
+            ffn_arrived(zi).wait_recv()
+        for kind in range(2):
+            side(kind, zi, 0).start()
+            side(kind, zi, 1).start()
+
+    for k in range(2):
+
+        @pl.when(foreign[k])
+        def _():
+            plane_copy(k, 0).wait_recv()
+            plane_copy(k, 2).start()
+            plane_copy(k, 1).wait_recv()
+            plane_copy(k, 3).start()
+
+    for d in range(head_count):
+        zi = (z + d) % head_count
+        side(0, zi, 0).wait_recv()
+        side(0, zi, 2).start()
+        side(1, zi, 1).wait_recv()
+        side(1, zi, 2).start()
+
+    locals_[0].wait()
+
+    @pl.when(is_home)
+    def _():
+        own_attention.wait()
+
+    for i in range(head_count - 1):
+        attention_out(i).wait_send()
+        ffn_out(i).wait_send()
+    for j in range(2):
+        for h in range(2):
+
+            @pl.when(jnp.logical_not((core == h) & (z == 2 * core + j)))
+            def _():
+                rows_out(j, h).wait_send()
+
+    for copy in pair:
+        copy.wait()
+    for k in range(2):
+
+        @pl.when(foreign[k])
+        def _():
+            plane_copy(k, 0).wait_send()
+            plane_copy(k, 1).wait_send()
+            plane_copy(k, 2).wait()
+            plane_copy(k, 3).wait()
+
+    for zs in range(head_count):
+        forward(zs).wait_send()
+        span = pl.ds((1 - core) * piece, piece)
+        push(rows_o.at[:, zs, span], rows_o.at[:, zs, span], fwd_s.at[zs], fwd_r.at[zs], sibling).wait_recv()
+
+    for d in range(head_count):
+        zi = (z + d) % head_count
+        for kind in range(2):
+            side(kind, zi, 0).wait_send()
+            side(kind, zi, 1).wait_send()
+        side(0, zi, 1).wait_recv()
+        side(1, zi, 0).wait_recv()
+        for kind in range(2):
+            side(kind, zi, 2).wait()
+
+    def small_in(i):
+        t = other(i)[0]
+        push(small, small_o.at[t], small_s.at[i], small_r.at[t], sibling).wait_recv()
+
+    loop(total - 1, lambda i: small_out(i).wait_send())
+    loop(total - 1, small_in)
+
+
+def finish_kernel(
+    dp_count, head_count,
+    fa, fb, at, y, dt,
+    fa_o, fb_o, at_o, y_o, dt_o,
+    fa_b, fb_b, at_b, fa_1, fa_2, fb_1, fb_2, at_1, at_2, fa_z, fb_z, at_z,
+    one_s, one_r, two_s, two_r, z_s, z_r, a_s, a_r, out_s, out_r, local_sem,
+):
+    core, px, py, z = place()
+    sibling = device(1 - core, px, py, z)
+    x_mate, y_mate = device(core, 1 - px, py, z), device(core, px, 1 - py, z)
+    far = [device(h, px, py, (z + 1 + i) % head_count) for h in range(2) for i in range(head_count - 1)]
+    greet([sibling, x_mate, y_mate] + far)
+
+    def add(dst, src):
+        count = dst.shape[0]
+
+        def run(i, unused):
+            dst[i] = (dst[i].astype(F32) + src[i].astype(F32)).astype(BF)
+            return unused
+
+        lax.fori_loop(0, count, run, 0)
+
+    piece = y_o.shape[2] // 2
+    block = y_o.shape[2]
+
+    def row_copy(which, zt):
+        src, dst = ((y, y_o), (dt, dt_o))[which]
+        span = pl.ds(core * piece, piece)
+        return src.at[:, pl.ds(pl.multiple_of(zt * block + core * piece, piece), piece)], dst.at[z % 2, :, span]
+
+    def row_out(which, i):
+        zt = (z + i) % head_count
+        src, dst = row_copy(which, zt)
+        return push(src, dst, out_s.at[which, i], out_r.at[which, z % 2, core], device(z // 2, px, py, zt))
+
+    def row_here(which):
+        src, dst = row_copy(which, z)
+        return pltpu.make_async_copy(src, dst, local_sem.at[which])
+
+    is_home = core == z // 2
+
+    def first(name, i):
+        if name == 0:
+            oy = 1 - py if i == 0 else py
+            return push(fa_b.at[oy, 1 - px], fa_1.at[i], one_s.at[0, i], one_r.at[0, i], x_mate)
+        if name == 1:
+            ox = 1 - px if i == 0 else px
+            return push(fb_b.at[1 - py, ox], fb_1.at[i], one_s.at[1, i], one_r.at[1, i], y_mate)
+        if name == 2:
+            oy = 1 - py if i == 0 else py
+            return push(at_b.at[0, oy, 1 - px], at_1.at[0, i], one_s.at[2, i], one_r.at[2, i], x_mate)
+        ox = 1 - px if i == 0 else px
+        return push(at_b.at[1, 1 - py, ox], at_1.at[1, i], one_s.at[3, i], one_r.at[3, i], y_mate)
+
+    def second(name):
+        if name == 0:
+            return push(fa_b.at[1 - py, px], fa_2, two_s.at[0], two_r.at[0], y_mate)
+        if name == 1:
+            return push(fb_b.at[py, 1 - px], fb_2, two_s.at[1], two_r.at[1], x_mate)
+        if name == 2:
+            return push(at_b.at[0, 1 - py, px], at_2.at[0], two_s.at[2], two_r.at[2], y_mate)
+        return push(at_b.at[1, py, 1 - px], at_2.at[1], two_s.at[3], two_r.at[3], x_mate)
+
+    def on_way(name):
+        return (fa_b.at[1 - py, px], fb_b.at[py, 1 - px], at_b.at[0, 1 - py, px], at_b.at[1, py, 1 - px])[name]
+
+    def kept(name):
+        return (fa_b.at[py, px], fb_b.at[py, px], at_b.at[0, py, px], at_b.at[1, py, px])[name]
+
+    def got_one(name, i):
+        return (fa_1.at[i], fb_1.at[i], at_1.at[0, i], at_1.at[1, i])[name]
+
+    def got_two(name):
+        return (fa_2, fb_2, at_2.at[0], at_2.at[1])[name]
+
+    loads = [
+        pltpu.make_async_copy(fa, fa_b, local_sem.at[3]),
+        pltpu.make_async_copy(fb, fb_b, local_sem.at[4]),
+        pltpu.make_async_copy(at, at_b, local_sem.at[5]),
+    ]
+    for copy in loads:
+        copy.start()
+    names = (0, 1, 2, 3)
+    for copy in loads:
+        copy.wait()
+    for i in range(2):
+        for name in names:
+            first(name, i).start()
+
+    for which in range(2):
+        for i in range(head_count):
+            if i == 0:
+
+                @pl.when(is_home)
+                def _():
+                    row_here(which).start()
+
+                @pl.when(jnp.logical_not(is_home))
+                def _():
+                    row_out(which, 0).start()
+
+            else:
+                row_out(which, i).start()
+
+    for name in names:
+        first(name, 0).wait_recv()
+        add(on_way(name), got_one(name, 0))
+        second(name).start()
+    for name in names:
+        first(name, 1).wait_recv()
+        add(kept(name), got_one(name, 1))
+
+    def z_out(name, i):
+        zt = (z + 1 + i) % head_count
+        buf, dst = ((fa_b, fa_z), (fb_b, fb_z))[name]
+        return push(buf.at[py, px, zt], dst.at[z], z_s.at[name, i], z_r.at[name, z], device(core, px, py, zt))
+
+    def z_in(name, i):
+        zs = (z + 1 + i) % head_count
+        buf, dst = ((fa_b, fa_z), (fb_b, fb_z))[name]
+        return push(buf.at[py, px, z], dst.at[zs], z_s.at[name, i], z_r.at[name, zs], sibling)
+
+    def a_out(k, h):
+        return push(
+            at_b.at[k, py, px, h], at_z.at[z], a_s.at[k, h], a_r.at[z], device(h, px, py, 2 * core + k)
+        )
+
+    def a_here(k):
+        return pltpu.make_async_copy(at_b.at[k, py, px, core], at_z.at[z], local_sem.at[2])
+
+    for name in names:
+        second(name).wait_recv()
+        add(kept(name), got_two(name))
+        if name < 2:
+            for i in range(head_count - 1):
+                z_out(name, i).start()
+        else:
+            k = name - 2
+            for h in range(2):
+                here = (core == h) & (z == 2 * core + k)
+
+                @pl.when(here)
+                def _():
+                    a_here(k).start()
+
+                @pl.when(jnp.logical_not(here))
+                def _():
+                    a_out(k, h).start()
+
+    for name in range(2):
+        for i in range(head_count - 1):
+            z_in(name, i).wait_recv()
+    for buf, got, out in ((fa_b, fa_z, fa_o), (fb_b, fb_z, fb_o)):
+        value = buf[py, px, z].astype(F32)
+        for i in range(head_count - 1):
+            value = value + got[(z + 1 + i) % head_count].astype(F32)
+        out[...] = value
+    for zs in range(head_count):
+        here = is_home & (z == zs)
+
+        @pl.when(here)
+        def _():
+            a_here(z % 2).wait()
+
+        @pl.when(jnp.logical_not(here))
+        def _():
+            push(at_b.at[0, 0, 0, 0], at_z.at[zs], a_s.at[0, 0], a_r.at[zs], sibling).wait_recv()
+
+    value = at_z[0].astype(F32)
+    for zs in range(1, head_count):
+        value = value + at_z[zs].astype(F32)
+    at_o[...] = value
+
+    for name in names:
+        for i in range(2):
+            first(name, i).wait_send()
+        second(name).wait_send()
+    for name in range(2):
+        for i in range(head_count - 1):
+            z_out(name, i).wait_send()
+    for k in range(2):
+        for h in range(2):
+
+            @pl.when(jnp.logical_not((core == h) & (z == 2 * core + k)))
+            def _():
+                a_out(k, h).wait_send()
+
+    for which in range(2):
+        for i in range(head_count):
+            if i == 0:
+
+                @pl.when(is_home)
+                def _():
+                    row_here(which).wait()
+
+                @pl.when(jnp.logical_not(is_home))
+                def _():
+                    row_out(which, 0).wait_send()
+
+            else:
+                row_out(which, i).wait_send()
+        src, dst = ((y, y_o), (dt, dt_o))[which]
+        for j in range(2):
+            for h in range(2):
+                span = pl.ds(h * piece, piece)
+
+                @pl.when(jnp.logical_not((core == h) & (z == 2 * core + j)))
+                def _():
+                    push(
+                        src.at[:, pl.ds(0, piece)], dst.at[j, :, span], out_s.at[which, 0],
+                        out_r.at[which, j, h], sibling,
+                    ).wait_recv()
+
+
+def vmem(shape, dtype=BF):
+    return pltpu.VMEM(shape, dtype)
+
+
+def sds(shape, dtype=BF):
+    return jax.ShapeDtypeStruct(shape, dtype)
+
+
+def dma(*shape):
+    return pltpu.SemaphoreType.DMA(shape)
+
+
+ANY = pl.BlockSpec(memory_space=pl.ANY)
+INV = pl.BlockSpec(memory_space=pltpu.VMEM)
+
+
+def by_chip(
+    text, boundary, reset, memory_in, init_memory, w_qkv, b_qv, w_out, w_in, w_back, b_in, norm_gains, biases,
+    cotangent,
+):
+    head_count = lax.axis_size("head")
+    dp_count = lax.axis_size("dp")
+    core = lax.axis_index("dp") % 2
+    z = lax.axis_index("head")
+    planes = dp_count // 2
+    total = dp_count * head_count
+    text_rows, width = text.shape[2], text.shape[3]
+    block = cotangent.shape[2]
+    seg_len = block * head_count
+    mem_rows = memory_in.shape[1]
+    local = w_qkv.shape[2]
+    hid = w_in.shape[1]
+    lanes = norm_gains.shape[1]
+    heads = 2 * local // HD
+    hidden = hid * planes * head_count
+
+    small = jnp.zeros((32, 128), BF)
+    small = small.at[0:16, 0:lanes].set(jnp.concatenate([norm_gains, biases, init_memory], axis=0))
+    small = small.at[16, 0:hid].set(b_in)
+    small = small.at[17:20].set(b_qv.reshape(3, 128))
+    j = z % 2
+    doc_ids = jnp.cumsum(boundary[j], axis=1).astype(F32)
+    marks = jnp.full((2, mem_rows), -1.0, F32)
+    labels = jnp.concatenate([marks, doc_ids, marks], axis=1)
+    flag_rows = jnp.broadcast_to(reset[j].astype(F32)[:, None], (2, seg_len))
+    seqf = jnp.concatenate([labels, flag_rows, jnp.zeros((4, seg_len), F32)], axis=0)
+    memp = jnp.pad(memory_in[j], ((0, 16 - mem_rows), (0, 0)))
+    text_pad = jnp.pad(text, ((0, 0), (0, 0), (0, block - text_rows), (0, 0)))
+    rows = jnp.concatenate([text_pad, cotangent], axis=1)
+    wa = jnp.concatenate([w_qkv.transpose(1, 2, 0).reshape(3 * local, width), w_out], axis=0)
+    wf = jnp.stack([w_in.T, w_back])
+
+    small_all, seq_pair, mem_pair, rows_all, wa_all, wf_all = pl.pallas_call(
+        functools.partial(start_kernel, dp_count, head_count),
+        out_shape=(
+            sds((total, 32, 128)),
+            sds((8, seg_len), F32),
+            sds((16, width)),
+            sds((4, head_count, block, width)),
+            sds((2, 4 * local, width)),
+            sds((2, planes * head_count, hid, width)),
+        ),
+        in_specs=[ANY] * 6,
+        out_specs=[ANY] * 6,
+        scratch_shapes=[
+            dma(total), dma(total), dma(2), dma(2), dma(2, 2), dma(4), dma(4), dma(4), dma(3), dma(2, 2),
+            dma(2, 4), dma(2, 4), dma(3), dma(4), dma(4, 2, 3), dma(4, 2, 3), dma(4),
+        ],
+        compiler_params=pltpu.CompilerParams(collective_id=0, has_side_effects=True),
+        name="start",
+    )(small, seqf, memp, rows, wa, wf)
+
+    home = core == z // 2
+    seqf = jnp.where(home, seqf, seq_pair)
+    mem_one = jnp.where(home, memp, mem_pair)
+    by_device = small_all.reshape(planes, 2, head_count, 32, 128)
+    vectors = by_device[:, :, :, 0:16, 0:lanes].transpose(3, 0, 1, 2, 4).reshape(16, width)
+    par = vectors.astype(F32)
+    own_core = lax.dynamic_index_in_dim(by_device, core, 1, keepdims=False)
+    bin_row = own_core[:, :, 16, 0:hid].reshape(1, hidden).astype(F32)
+    qv = lax.dynamic_slice_in_dim(own_core[0], 2 * core, 2, 0)[:, 17:20].reshape(2, 2, local).astype(F32)
+    bqv = jnp.concatenate([qv[:, 0], jnp.zeros((2, local), F32), qv[:, 1]], axis=1)[:, :, None]
+    init = vectors[6 : 6 + mem_rows]
+    init_a = jnp.pad(init, ((0, 16 - mem_rows), (0, 0)))
+    init_b = jnp.pad(init, ((16 - mem_rows, 0), (0, 0)))
+    flags = jnp.broadcast_to(seqf[2:4, 0:1], (2, width))
+    flags = jnp.concatenate([flags, jnp.zeros((6, width), F32)], axis=0)
+    mem_a = jnp.where(flags[0:1] > 0, init_a, mem_one)
+    mem_b = jnp.roll(mem_a, 16 - mem_rows, axis=0)
+    lab_row = seqf[0:2, None, :]
+    lab_col = seqf[0:2, :, None]
+    rows_nat = rows_all.reshape(4, seg_len, width)
+    wf_nat = wf_all.reshape(2, hidden, width)
+
+    y, dt, ffg, agq, ago, sg, dinit, dbin, dbqv = pl.pallas_call(
+        functools.partial(layer_kernel, mem_rows),
+        out_shape=(
+            sds((2, seg_len, width)),
+            sds((2, seg_len, width)),
+            sds((2, hidden, width)),
+            sds((2, width, 3 * local)),
+            sds((2, width, local)),
+            sds((8, width), F32),
+            sds((16, width), F32),
+            sds((8, hidden), F32),
+            sds((2, 3 * local, 1), F32),
+        ),
+        in_specs=[INV] * 13,
+        out_specs=[INV, INV, ANY] + [INV] * 6,
+        scratch_shapes=[
+            vmem((2, seg_len, width)),
+            vmem((2, 2, 3 * local, seg_len)),
+            vmem((2, heads, seg_len, seg_len)),
+            vmem((2, 2, local, seg_len)),
+            vmem((seg_len, seg_len), F32),
+            vmem((seg_len, width), F32),
+            vmem((seg_len, width), F32),
+            vmem((2, seg_len, width)),
+            vmem((2, seg_len, 1), F32),
+            vmem((2, seg_len, width)),
+            vmem((2, seg_len, hidden)),
+            vmem((2, seg_len, hidden)),
+            vmem((2, seg_len, width)),
+            vmem((2, seg_len, 1), F32),
+            vmem((2, seg_len, width)),
+            vmem((2, seg_len, hidden)),
+            vmem((2, seg_len, width)),
+            vmem((2, local, seg_len)),
+            vmem((2, 2, 3 * local, seg_len)),
+            vmem((2, 4, 128, width)),
+            vmem((2, 4, 128, width)),
+            vmem((16, width)),
+            vmem((16, width)),
+            vmem((128, width), F32),
+            vmem((2, 256, width)),
+            dma(2, 4),
+            dma(2, 4),
+            dma(2),
+        ],
+        compiler_params=pltpu.CompilerParams(
+            collective_id=1, has_side_effects=True, vmem_limit_bytes=VMEM_LIMIT
+        ),
+        name="layer",
+    )(rows_nat, wa_all, wf_nat, lab_row, lab_col, par, bqv, bin_row, mem_a, mem_b, init_a, init_b, flags)
+
+    vec = jnp.concatenate([sg[0:6], dinit[16 - mem_rows : 16]], axis=0)
+    vec = vec.reshape(16, planes, 2, head_count, lanes)
+    vec = lax.dynamic_index_in_dim(vec, core, 2, keepdims=False).transpose(1, 2, 0, 3)
+    bin_part = jnp.pad(
+        dbin[0].reshape(planes, head_count, 1, hid), ((0, 0), (0, 0), (0, 15), (128, width - 128 - hid))
+    )
+    vec = jnp.pad(vec, ((0, 0), (0, 0), (0, 0), (0, width - lanes))) + bin_part
+    ffg = ffg.reshape(2, planes, head_count, hid, width)
+    fa = jnp.concatenate([ffg[0], vec.astype(BF)], axis=2)
+    dqv = jnp.stack([dbqv[:, 0:local, 0], dbqv[:, 2 * local :, 0]], axis=1)
+    slice_b = HD // dp_count
+    dqv = dqv.reshape(2, 2, local // HD, dp_count, slice_b).transpose(0, 3, 1, 2, 4)
+    dqv = dqv.reshape(2, dp_count, 1, -1)
+    dqv = jnp.pad(dqv, ((0, 0), (0, 0), (0, 15), (0, width - dqv.shape[3])))
+    share = width // dp_count
+    att = jnp.concatenate([agq, ago], axis=2).reshape(2, dp_count, share, width)
+    att = jnp.concatenate([att, dqv.astype(BF)], axis=2)
+    plane_shape = (2, 2)
+    fa = fa.reshape(plane_shape + fa.shape[1:])
+    fb = ffg[1].reshape(plane_shape + ffg.shape[2:])
+    att = att.reshape((2,) + plane_shape + (2,) + att.shape[2:])
+    hc, ra, rb, rt = head_count, hid + 16, hid, share + 16
+
+    fa_o, fb_o, at_o, acts, grad_text = pl.pallas_call(
+        functools.partial(finish_kernel, dp_count, head_count),
+        out_shape=(
+            sds((ra, width), F32),
+            sds((rb, width), F32),
+            sds((rt, width), F32),
+            sds((2, 2, block, width)),
+            sds((2, 2, block, width)),
+        ),
+        in_specs=[ANY] * 5,
+        out_specs=[INV, INV, INV, ANY, ANY],
+        scratch_shapes=[
+            vmem((2, 2, hc, ra, width)),
+            vmem((2, 2, hc, rb, width)),
+            vmem((2, 2, 2, 2, rt, width)),
+            vmem((2, hc, ra, width)),
+            vmem((hc, ra, width)),
+            vmem((2, hc, rb, width)),
+            vmem((hc, rb, width)),
+            vmem((2, 2, 2, rt, width)),
+            vmem((2, 2, rt, width)),
+            vmem((hc, ra, width)),
+            vmem((hc, rb, width)),
+            vmem((hc, rt, width)),
+            dma(4, 2), dma(4, 2), dma(4), dma(4), dma(2, 3), dma(2, 4), dma(2, 2), dma(4), dma(2, 4),
+            dma(2, 2, 2), dma(6),
+        ],
+        compiler_params=pltpu.CompilerParams(
+            collective_id=2, has_side_effects=True, vmem_limit_bytes=VMEM_LIMIT
+        ),
+        name="finish",
+    )(fa, fb, att, y, dt)
+
+    d_vec = fa_o[hid:, 0:lanes]
+    d_bqv = at_o[share, 0 : 2 * (local // HD) * slice_b].reshape(2, local // HD, slice_b)
+    return (
+        acts,
+        grad_text[:, :, 0:text_rows],
+        d_vec[6:16],
+        at_o[:share, 0 : 3 * local].reshape(share, 3, local),
+        d_bqv,
+        at_o[:share, 3 * local :].T,
+        fa_o[:hid].T,
+        fb_o,
+        fa_o[hid, 128 : 128 + hid],
+        d_vec[0:2],
+        d_vec[2:6],
+    )
+
+
 def solution(mesh):
+    body = by_chip if mesh.shape["dp"] == 8 and mesh.shape["head"] == 4 else local
     return jax.shard_map(
-        local,
+        body,
         mesh=mesh,
         in_specs=(
             P("dp", None, "head", None),

time: 1050 us -> 370 us (0.35)
  waiting for transfers between devices: 478 us -> 0 us
  blocking collectives: 323 us -> 0 us
  Pallas kernels: 0 us -> 314 us
  matrix products: 98.1 us -> 0 us
  local copies, waits for them, and re-layouts: 75 us -> 35.9 us
  other arithmetic: 47.8 us -> 14.2 us
  between operations: 20.2 us -> 1.7 us
    pallas_call x0 -> x3, Pallas kernels: none -> 314 us  [the longest x1 113 us: by_chip(): pl.pallas_call(functools.partial(start_kernel, dp_count, head_count), out...]
    reduce_scatter x7 -> x0, waiting for transfers between devices: 263 us -> none  [the longest x1 85 us: local(): lax.psum_scatter(ffn_total[0].astype(jnp.bfloat16), 'head', scatter_dimen...]
    all_gather x3 -> x0, blocking collectives: 202 us -> none  [the longest x1 73 us: local(): lax.all_gather(init_memory, ('dp', 'head'), axis=1, tiled=True)]
    unnamed x23 -> x0, waiting for transfers between devices: 180 us -> none
    dot_general x36 -> x0, matrix products: 98.1 us -> none  [the longest x2 10.7 us: backward(): jnp.einsum('srd,fd->srf', grad_outer, w_back_all, preferred_element_type=...]
    unnamed x2 -> x0, blocking collectives: 62.3 us -> none
    psum x3 -> x0, blocking collectives: 58.2 us -> none  [the longest x2 39.8 us: backward(): lax.psum((grad_rows[:, :mem_rows] + grad_rows[:, seg_len - mem_rows:]).as...]
    all_gather x6 -> x0, waiting for transfers between devices: 34.5 us -> none  [the longest x2 34.4 us: backward(): lax.all_gather(grad_pre.astype(jnp.bfloat16), 'head', axis=1, tiled=True)]
  transfers between devices with their start and end apart: 18 -> 0, of which waited for: 12 -> 0; matrix products, arithmetic and copies ran while one was open for 13% -> 0% of each run, Pallas kernels for 0% -> 0%
where the time goes in v1:
time: 370 us; the launch traced here: 366 us
  Pallas kernels  314 us (85%)
  local copies, waits for them, and re-layouts  35.9 us (10%)
  other arithmetic  14.2 us (4%)
    pallas_call x1, Pallas kernels, by_chip(): pl.pallas_call(functools.partial(start_kernel, dp_count, head_count), out...  113 us
    pallas_call x1, Pallas kernels, by_chip(): pl.pallas_call(functools.partial(finish_kernel, dp_count, head_count), ou...  111 us
    pallas_call x1, Pallas kernels, by_chip(): pl.pallas_call(functools.partial(layer_kernel, mem_rows), out_shape=(sds(...  90.3 us
    unnamed x34, local copies, waits for them, and re-layouts  9.31 us

profile of v1, /device:TPU:0, one launch (start us, length us, event | category | flops | bytes accessed | tf_op | source)
XLA Modules:
  0.0 365.9 jit_solution(257438813424108714)
XLA Ops:
  0.7 0.8 fusion.12
  1.6 0.7 copy.37
  2.3 0.1 reshape.199
  2.5 0.7 dynamic-slice_bitcast_fusion.1
  3.2 0.6 reduce-window.6
  3.8 0.2 slice_reduce_fusion.3
  4.0 0.2 reduce-window.9
  4.3 0.7 fusion.10
  5.0 0.8 scatter.11
  5.8 0.1 scatter.14.small
  5.9 0.7 maximum_maximum_fusion.seqf
  6.6 0.8 constant_dynamic-slice_fusion.2
  7.4 0.6 pad.44.memp
  8.0 1.7 pad_maximum_fusion.4.wf
  9.8 1.3 copy.39
  11.1 1.3 fusion.1.rows
  12.4 1.1 pad_maximum_fusion.3.wa
  13.5 112.7 %start.1 = (bf16[32,32,128]{2,1,0:T(8,128)(2,1)}, f32[8,512]{1,0:T(8,128)}, bf16[16,768]{1,0:T(8,128)(2,1)}, bf16[4,4,128,768]{3,2,1,0:T(8,128)(2,1)}, bf16[2,76...) custom-call(bf16[32,128]{1,0:T(8,128)(2,1)} %copy-done.10, f32[8,512]{1,0:T(8,128)} %maximum_maximum_fusion.seqf, ...), custom_call_target="tpu_custom_call" | custom-call | tf_op jit(solution)/shard_map/start/pallas_call | solution.py:1189
  126.2 0.1 broadcast_select_fusion
  126.3 0.5 slice.207
  127.5 0.1 slice_reduce_fusion.4
  127.6 0.6 broadcast_in_dim.38.lab_row
  128.2 0.7 dynamic-slice_bitcast_fusion
  128.9 0.1 reshape.210
  129.1 0.7 concatenate.65.flags
  129.7 0.9 constant_dynamic-slice_fusion.1
  130.6 0.9 slice.202
  131.7 0.7 reshape.211.bin_ref
  132.3 0.1 copy_bitcast_fusion
  132.5 0.2 slice.179
  132.6 0.6 fusion.15
  133.3 0.6 copy-done.6
  133.9 0.6 pad_maximum_fusion.6.mem_b
  134.5 0.9 reshape.209.par
  135.4 1.0 copy.43.lab_col
  136.4 1.1 copy.44.bqv
  137.4 90.3 %layer.1 = (bf16[2,512,768]{2,1,0:T(8,128)(2,1)}, bf16[2,512,768]{2,1,0:T(8,128)(2,1)}, bf16[2,1536,768]{2,1,0:T(8,128)(2,1)}, bf16[2,768,576]{2,1,0:T(8,128)(2,...) custom-call(bf16[4,512,768]{2,1,0:T(8,128)(2,1)} %bitcast.71, ...), custom_call_target="tpu_custom_call" | custom-call | tf_op jit(solution)/shard_map/layer/pallas_call | solution.py:1231
  227.7 4.1 %fusion.14 = (bf16[1,1536,768]{2,1,0:T(8,128)(2,1)}, bf16[1,1536,768]{2,1,0:T(8,128)(2,1)S(1)}) fusion(bf16[2,1536,768]{2,1,0:T(8,128)(2,1)} %get-tuple-element.73), kind=kLoop, calls=%fused_computation.57 | loop fusion | bytes 9437184 | tf_op jit(solution)/shard_map/slice | solution.py:1301
  231.8 0.8 slice_reduce_fusion.2
  232.6 0.1 reshape_squeeze.10
  232.8 0.4 reshape.206
  233.3 1.7 pad_maximum_fusion.fa
  235.1 0.2 slice_reduce_fusion.1
  235.2 0.1 stack.19
  235.3 0.1 stack.20
  235.5 0.1 reshape.217
  235.6 2.0 pad_maximum_fusion.2
  237.6 1.8 pad_maximum_fusion.1.at
  239.4 111.1 %finish.1 = (f32[112,768]{1,0:T(8,128)}, f32[96,768]{1,0:T(8,128)}, f32[112,768]{1,0:T(8,128)}, bf16[2,2,128,768]{3,2,1,0:T(8,128)(2,1)}, bf16[2,2,128,768]{3,2,1,0:T(8,128)(2,1)}) custom-call(bf16[2,2,4,112,768]{4,3,2,1,0:T(8,128)(2,1)} %pad_maximum_fusion.fa, bf16[2,2,4,96,768]{4,3,2,1,0:T(8,128)(2,1)} %bitcast.68, ...), custom_call_target="tpu_custom_call" | custom-call | tf_op jit(solution)/shard_map/finish/pallas_call | solution.py:1305
  350.6 2.9 copy.50
  353.4 0.7 slice_reduce_fusion.5
  354.2 1.2 slice_bitcast_fusion.2
  355.4 1.2 slice.197
  356.6 1.3 slice.198
  357.9 0.1 reshape_squeeze.12
  357.9 0.6 copy.52
  358.5 1.3 slice.191
  359.8 1.7 slice_bitcast_fusion
  361.5 1.0 slice_bitcast_fusion.1
  362.5 0.7 copy.53
  363.3 0.1 copy.49
  363.4 0.9 copy.51
  364.3 0.9 copy.77
  365.2 0.7 copy.78
  (55 shorter events, 0.8 us)
Async XLA Ops:
  0.6 10.4 %copy-start.3 = (bf16[2,2,128,768]{3,2,1,0:T(8,128)(2,1)S(1)}, bf16[2,2,128,768]{3,2,1,0:T(8,128)(2,1)}, u32[]{:S(2)}) copy-start(bf16[2,2,128,768]{3,2,1,0:T(8,128)(2,1)} %param.33) | copy-start | bytes 2359300
  5.9 6.5 %copy-start.10 = (bf16[32,128]{1,0:T(8,128)(2,1)}, bf16[32,128]{1,0:T(8,128)(2,1)S(1)}, u32[]{:S(2)}) copy-start(bf16[32,128]{1,0:T(8,128)(2,1)S(1)} %scatter.14.small) | copy-start | bytes 24580
  9.8 2.6 copy-start
  9.8 2.6 copy-start.7
  133.3 0.6 copy-start.6
  227.7 5.0 %copy-start.9 = (f32[16,768]{1,0:T(8,128)S(1)}, f32[16,768]{1,0:T(8,128)}, u32[]{:S(2)}) copy-start(f32[16,768]{1,0:T(8,128)} %get-tuple-element.75) | copy-start | bytes 147460
  227.7 5.0 %copy-start.11 = (f32[8,768]{1,0:T(8,128)S(1)}, f32[8,768]{1,0:T(8,128)}, u32[]{:S(2)}) copy-start(f32[8,768]{1,0:T(8,128)} %get-tuple-element.74) | copy-start | bytes 73732
  233.3 1.8 copy-start.4
  233.3 2.3 copy-start.1
  350.5 12.0 %copy-start.5 = (f32[112,768]{1,0:T(8,128)S(1)}, f32[112,768]{1,0:T(8,128)}, u32[]{:S(2)}) copy-start(f32[112,768]{1,0:T(8,128)} %get-tuple-element.85) | copy-start | bytes 1032196
  350.6 13.8 %copy-start.2 = (bf16[2,2,128,768]{3,2,1,0:T(8,128)(2,1)S(1)}, bf16[2,2,128,768]{3,2,1,0:T(8,128)(2,1)}, u32[]{:S(2)}) copy-start(bf16[2,2,128,768]{3,2,1,0:T(8,128)(2,1)} %get-tuple-element.135) | copy-start | bytes 2359300
  353.4 11.8 %copy-start.8 = (f32[96,768]{1,0:T(8,128)S(1)}, f32[96,768]{1,0:T(8,128)}, u32[]{:S(2)}) copy-start(f32[96,768]{1,0:T(8,128)} %get-tuple-element.142) | copy-start | bytes 884740

commit v2 on v0

--- a/solution.py
+++ b/solution.py
@@ -1,9 +1,45 @@
+import functools
+
 import jax
 import jax.numpy as jnp
 from jax import lax
+from jax.experimental import pallas as pl
+from jax.experimental.pallas import tpu as pltpu
 from jax.sharding import PartitionSpec as P
 
 HD = 64
+MESH = pl.DeviceIdType.MESH
+BF = jnp.bfloat16
+F32 = jnp.float32
+VMEM_LIMIT = 64 * 1024 * 1024
+
+
+def nn(a, b):
+    return lax.dot_general(a, b, (((1,), (0,)), ((), ())), preferred_element_type=F32)
+
+
+def nt(a, b):
+    return lax.dot_general(a, b, (((1,), (1,)), ((), ())), preferred_element_type=F32)
+
+
+def tn(a, b):
+    return lax.dot_general(a, b, (((0,), (0,)), ((), ())), preferred_element_type=F32)
+
+
+def place():
+    dp, z = lax.axis_index("dp"), lax.axis_index("head")
+    core, plane = dp % 2, dp // 2
+    return core, plane % 2, plane // 2, z
+
+
+def device(core, x, y, z):
+    return ((y * 2 + x) * 2 + core, z)
+
+
+def push(src, dst, send, recv, target):
+    return pltpu.make_async_remote_copy(
+        src_ref=src, dst_ref=dst, send_sem=send, recv_sem=recv, device_id=target, device_id_type=MESH
+    )
 
 
 def from_root(x, axis, root):
@@ -329,9 +365,1201 @@
     )
 
 
+class Refs:
+    pass
+
+
+def by_name(names, values):
+    refs = Refs()
+    for name, value in zip(names, values, strict=True):
+        setattr(refs, name, value)
+    return refs
+
+
+def loop(count, body):
+    def run(i, unused):
+        body(i)
+        return unused
+
+    lax.fori_loop(0, count, run, 0)
+
+
+def add_blocks(dst, src):
+    def body(i):
+        dst[i] = (dst[i].astype(F32) + src[i].astype(F32)).astype(BF)
+
+    loop(dst.shape[0], body)
+
+
+def add_block(dst, src):
+    dst[...] = (dst[...].astype(F32) + src[...].astype(F32)).astype(BF)
+
+
+def as_column(row):
+    n = row.shape[1]
+    down = lax.broadcasted_iota(jnp.int32, (n, n), 0)
+    across = lax.broadcasted_iota(jnp.int32, (n, n), 1)
+    return jnp.sum(jnp.where(down == across, row, 0.0), axis=1, keepdims=True)
+
+
+def norm(v):
+    center = v - jnp.mean(v, axis=-1, keepdims=True)
+    scale = lax.rsqrt(jnp.mean(center * center, axis=-1, keepdims=True) + 1e-05)
+    return center * scale, scale
+
+
+def pull_norm(g, hat, scale):
+    m1 = jnp.mean(g, axis=-1, keepdims=True)
+    m2 = jnp.mean(g * hat, axis=-1, keepdims=True)
+    return scale * (g - m1 - hat * m2)
+
+
+def row_sum(v):
+    return jnp.sum(v, axis=0, keepdims=True)
+
+
+def main_kernel(names, dp_count, head_count, *values):
+    r_ = by_name(names, values)
+    core, px, py, z = place()
+    plane = py * 2 + px
+    x_plane, y_plane = py * 2 + 1 - px, (1 - py) * 2 + px
+    me = (plane * 2 + core) * head_count + z
+    total = dp_count * head_count
+    planes = dp_count // 2
+    is_home = core == z // 2
+    away = jnp.logical_not(is_home)
+    sibling = device(1 - core, px, py, z)
+    x_mate, y_mate = device(core, 1 - px, py, z), device(core, px, 1 - py, z)
+    mirror = z // 2
+
+    def from_end(i):
+        return i + mirror * (head_count - 1 - 2 * i)
+
+    depth = from_end(z)
+    inside = depth == 1
+    order = [from_end(i) for i in (depth, 1 - depth, 2, 3)]
+
+    x, qkv, pt, ot, wa, wf = r_.x, r_.qkv, r_.pt, r_.ot, r_.wa, r_.wf
+    hf, acc, par = r_.hf, r_.acc, r_.par
+    seg_len, width = x.shape[1], x.shape[2]
+    hidden = r_.u.shape[2]
+    heads = pt.shape[1]
+    local = ot.shape[2]
+    hid = r_.w_back.shape[0]
+    lanes = r_.norm_gains.shape[1]
+    mem_rows = r_.memory_in.shape[0]
+    text_rows = r_.text.shape[2]
+    per_block = local // HD
+    step = seg_len // head_count
+    piece = step // 2
+    chunk = hidden // head_count
+    tail = 16
+
+    def rows(r):
+        return pl.ds(pl.multiple_of(r * step, step), step)
+
+    def cols(i):
+        return pl.ds(pl.multiple_of(i * chunk, chunk), chunk)
+
+    def head_rows(h, part):
+        return pl.ds(pl.multiple_of((h % per_block) * HD + part * local, HD), HD)
+
+    def column(i):
+        h = core if i < head_count - 1 else 1 - core
+        zt = (z + 1 + i) % head_count
+        return (plane * 2 + h) * head_count + zt, device(h, px, py, zt)
+
+    column_size = 2 * head_count - 1
+
+    def when_not(cond, body):
+        pl.when(jnp.logical_not(cond))(body)
+
+    share = local
+    half = share // 2
+
+    def attention_out(i, which):
+        zt = (z + 1 + i) % head_count
+        at = pl.multiple_of((share * jnp.minimum(plane, planes - 2) if which == 0 else 0) + half * core, half)
+        src = (r_.wq_t, r_.w_out)[which]
+        return push(
+            src.at[pl.ds(at, half)], wa.at[z % 2, pl.ds(pl.multiple_of(share * plane + half * core, half), half)],
+            r_.att_s.at[i], r_.att_r.at[z % 2, core], device(z // 2, px, py, zt),
+        )
+
+    def attention_outs(do):
+        for which, mine in enumerate((plane < planes - 1, plane == planes - 1)):
+
+            def each():
+                for i in range(head_count - 1):
+                    do(attention_out(i, which))
+
+            pl.when(mine)(each)
+
+    def attention_in(k, h):
+        span = pl.ds(pl.multiple_of(share * plane + half * h, half), half)
+        return push(r_.w_out.at[pl.ds(0, half)], wa.at[k, span], r_.att_s.at[0], r_.att_r.at[k, h], sibling)
+
+    def attention_plane(k, which):
+        at, count, mate = (
+            (share * plane, share, x_mate),
+            (share * plane, share, y_mate),
+            (share * x_plane, half, y_mate),
+            (share * y_plane + half, half, x_mate),
+        )[which]
+        block = pl.ds(pl.multiple_of(at, half), count)
+        return push(
+            wa.at[k, block], wa.at[k, block], r_.plane_s.at[k, which], r_.plane_r.at[k, which], mate
+        )
+
+    own_attention = [
+        pltpu.make_async_copy(r_.wq_t, wa.at[z % 2, pl.ds(0, 3 * local)], r_.local_sem.at[0]),
+        pltpu.make_async_copy(r_.w_out, wa.at[z % 2, pl.ds(3 * local, local)], r_.local_sem.at[1]),
+    ]
+    foreign = [jnp.logical_not(is_home & (z % 2 == k)) for k in range(2)]
+
+    def rows_src(a, j, h):
+        src = r_.text_pad if a < 2 else r_.cotangent
+        return src.at[j, a % 2, pl.ds(h * piece, piece)]
+
+    def rows_dst(a, zs, h):
+        dst = r_.text_all if a < 2 else r_.cot_all
+        return dst.at[a % 2, pl.ds(pl.multiple_of(zs * step + h * piece, piece), piece)]
+
+    def rows_out(a, j, h):
+        return push(
+            rows_src(a, j, h), rows_dst(a, z, h), r_.rows_s.at[a, j, h], r_.rows_r.at[a, z],
+            device(h, px, py, 2 * core + j),
+        )
+
+    def rows_here(a, j, h):
+        return pltpu.make_async_copy(rows_src(a, j, h), rows_dst(a, z, h), r_.here_sem.at[a])
+
+    def rows_send(a):
+        for j in range(2):
+            for h in range(2):
+                here = (core == h) & (z == 2 * core + j)
+                pl.when(here)(lambda: rows_here(a, j, h).start())
+                when_not(here, lambda: rows_out(a, j, h).start())
+
+    def rows_forward(a, zs, h):
+        ref = rows_dst(a, zs, h)
+        return push(ref, ref, r_.fwd_s.at[a, zs], r_.fwd_r.at[a, zs], sibling)
+
+    def rows_pass(a):
+        for zs in range(head_count):
+            here = is_home & (z == zs)
+            pl.when(here)(lambda: rows_here(a, z % 2, core).wait())
+            when_not(
+                here,
+                lambda: push(
+                    rows_src(a, 0, 0), rows_dst(a, zs, core), r_.rows_s.at[a, 0, 0], r_.rows_r.at[a, zs], sibling
+                ).wait_recv(),
+            )
+            rows_forward(a, zs, core).start()
+
+    def rows_ready(a):
+        for zs in range(head_count):
+            rows_forward(a, zs, 1 - core).wait_recv()
+
+    def rows_done(a):
+        for j in range(2):
+            for h in range(2):
+                when_not((core == h) & (z == 2 * core + j), lambda: rows_out(a, j, h).wait_send())
+        for zs in range(head_count):
+            rows_forward(a, zs, core).wait_send()
+
+    def hidden_block(p, zi):
+        return pl.ds(pl.multiple_of((zi * planes + p) * hid, hid), hid)
+
+    def ffn_push(zi, to, slot):
+        ref = wf.at[:, hidden_block(plane, zi)]
+        return push(ref, ref, r_.ffn_s.at[slot], r_.ffn_r.at[zi], device(core, px, py, to))
+
+    ffn_hops = [(0, from_end(1 - depth)), (0, from_end(2)), (1, from_end(2)), (2, from_end(0)), (3, from_end(0))]
+
+    def ffn_hop(i):
+        which, to = ffn_hops[i]
+        return ffn_push(order[which], to, i)
+
+    def ffn_own():
+        ffn_hop(0).start()
+        pl.when(inside)(ffn_hop(1).start)
+
+    def ffn_one(n):
+        ffn_push(order[n], z, 0).wait_recv()
+        pl.when(inside)(ffn_hop(n + 1).start)
+        side_first(order[n])
+
+    def ffn_sent():
+        ffn_hop(0).wait_send()
+
+        def rest():
+            for i in range(1, 5):
+                ffn_hop(i).wait_send()
+
+        pl.when(inside)(rest)
+
+    def side(kind, zi, which):
+        p, mate = (
+            (plane, x_mate),
+            (plane, y_mate),
+            (x_plane, y_mate) if kind == 0 else (y_plane, x_mate),
+        )[which]
+        ref = wf.at[kind, hidden_block(p, zi)]
+        return push(ref, ref, r_.side_s.at[zi, kind, which], r_.side_r.at[zi, kind, which], mate)
+
+    def side_first(zi):
+        for kind in range(2):
+            side(kind, zi, 0).start()
+            side(kind, zi, 1).start()
+
+    def ffn_two(n):
+        zi = order[n]
+        side(0, zi, 0).wait_recv()
+        side(0, zi, 2).start()
+        side(1, zi, 1).wait_recv()
+        side(1, zi, 2).start()
+
+    def ffn_ready(n):
+        zi = order[n]
+        side(0, zi, 1).wait_recv()
+        side(1, zi, 0).wait_recv()
+        side(0, zi, 2).wait_recv()
+        side(1, zi, 2).wait_recv()
+
+    def small_out(i):
+        return push(r_.small, r_.small_all.at[me], r_.small_s.at[i], r_.small_r.at[z, core], column(i)[1])
+
+    def small_in(i):
+        at, (dp_i, z_i) = column(i)
+        return push(r_.small, r_.small_all.at[at], r_.small_s.at[i], r_.small_r.at[z_i, dp_i % 2], sibling)
+
+    def small_plane(i):
+        p, mate = ((plane, x_mate), (plane, y_mate), (x_plane, y_mate))[i]
+        ref = r_.small_all.at[pl.ds(p * 2 * head_count, 2 * head_count)]
+        return push(ref, ref, r_.small_ps.at[i], r_.small_pr.at[i], mate)
+
+    pair = [
+        push(r_.seqf, r_.seqf_in, r_.pair_s.at[0], r_.pair_r.at[0], sibling),
+        push(r_.memp, r_.memp_in, r_.pair_s.at[1], r_.pair_r.at[1], sibling),
+    ]
+
+    barrier = pltpu.get_barrier_semaphore()
+    mates = [x_mate, y_mate] + [column(i)[1] for i in range(column_size)]
+    for mate in mates:
+        pl.semaphore_signal(barrier, inc=1, device_id=mate, device_id_type=MESH)
+    for j in range(2):
+        for s in range(2):
+            r_.text_pad[j, s, 0:text_rows, :] = r_.text[j, s]
+            r_.text_pad[j, s, text_rows:step, :] = jnp.zeros((step - text_rows, width), BF)
+    wf[0, hidden_block(plane, z), :] = r_.w_in_t[...]
+    wf[1, hidden_block(plane, z), :] = r_.w_back[...]
+    vtmp = r_.vtmp
+    vtmp[...] = jnp.zeros_like(vtmp)
+    vtmp[0:2, 0:lanes] = r_.norm_gains[...].astype(F32)
+    vtmp[2:6, 0:lanes] = r_.biases[...].astype(F32)
+    vtmp[6 : 6 + mem_rows, 0:lanes] = r_.init_memory[...].astype(F32)
+    vtmp[0:1, 32 : 32 + hid] = r_.b_in[...].astype(F32)
+    for b in range(per_block):
+        pair_b = r_.b_qv[b].astype(F32)
+        for part in range(2):
+            vtmp[1 + part * per_block + b : 2 + part * per_block + b, 32 : 32 + HD] = pair_b[part : part + 1, :]
+    r_.small[...] = vtmp[...].astype(BF)
+    r_.small_all[me] = r_.small[...]
+    seqf = r_.seqf
+    marks = r_.boundary[z % 2].astype(F32).astype(BF)
+    text_len = marks.shape[1]
+    n_from = lax.broadcasted_iota(jnp.int32, (text_len, seg_len), 0)
+    n_to = lax.broadcasted_iota(jnp.int32, (text_len, seg_len), 1) - mem_rows
+    counts = nn(marks, jnp.where(n_from <= n_to, 1.0, 0.0).astype(BF))
+    at_row = lax.broadcasted_iota(jnp.int32, (2, seg_len), 1)
+    seqf[...] = jnp.zeros_like(seqf)
+    seqf[0:2, :] = jnp.where((at_row >= mem_rows) & (at_row < seg_len - mem_rows), counts, -1.0)
+    for s in range(2):
+        seqf[2 + s : 3 + s, :] = jnp.full((1, seg_len), r_.reset[z % 2, s].astype(F32))
+    r_.memp[...] = jnp.zeros_like(r_.memp)
+    both_in = r_.memory_in[...].astype(F32)
+    r_.memp[0:mem_rows, :] = jnp.where(z % 2 == 0, both_in[:, 0, :], both_in[:, 1, :]).astype(BF)
+    for ref in (r_.sg, r_.dinit, r_.dbin, r_.carry):
+        ref[...] = jnp.zeros_like(ref)
+    pl.semaphore_wait(barrier, len(mates))
+
+    attention_outs(lambda c: c.start())
+
+    def keep_own():
+        for copy in own_attention:
+            copy.start()
+
+    pl.when(is_home)(keep_own)
+    rows_send(0)
+    for i in range(column_size):
+        small_out(i).start()
+    for copy in pair:
+        copy.start()
+    side_first(z)
+
+    def attention_to_plane(k):
+        for h in range(2):
+            attention_in(k, h).wait_recv()
+        attention_plane(k, 0).start()
+        attention_plane(k, 1).start()
+
+    def attention_across(k):
+        attention_plane(k, 0).wait_recv()
+        attention_plane(k, 2).start()
+        attention_plane(k, 1).wait_recv()
+        attention_plane(k, 3).start()
+
+    for i in range(column_size):
+        small_in(i).wait_recv()
+    small_plane(0).start()
+    small_plane(1).start()
+    for k in range(2):
+        pl.when(foreign[k])(lambda: attention_to_plane(k))
+    ffn_own()
+    small_plane(0).wait_recv()
+    small_plane(2).start()
+    ffn_two(0)
+    rows_pass(0)
+    for k in range(2):
+        pl.when(foreign[k])(lambda: attention_across(k))
+
+    for copy in pair:
+        copy.wait_recv()
+    small_plane(1).wait_recv()
+    small_plane(2).wait_recv()
+    for i in range(total):
+        par[0:16, lanes * i : lanes * (i + 1)] = r_.small_all[i, 0:16, 0:lanes].astype(F32)
+    for zi in range(head_count):
+        for p in range(planes):
+            at = (zi * planes + p) * hid
+            line = r_.small_all[(2 * p + core) * head_count + zi].astype(F32)
+            r_.bin_row[0:1, at : at + hid] = line[0:1, 32 : 32 + hid]
+    r_.bqv[...] = jnp.zeros_like(r_.bqv)
+    for k in range(2):
+        lines = r_.small_all[2 * core + k].astype(F32)
+        for part in range(2):
+            for b in range(per_block):
+                line = lines[1 + part * per_block + b : 2 + part * per_block + b, 32 : 32 + HD]
+                at = 2 * part * local + b * HD
+                r_.bqv[k, at : at + HD, :] = as_column(line)
+    seq = jnp.where(is_home, seqf[...], r_.seqf_in[...])
+    seqf_out = r_.seq
+    seqf_out[...] = seq
+    flags = [seqf_out[2 + s : 3 + s, 0:1] for s in range(2)]
+    tail_row = lax.broadcasted_iota(jnp.int32, (tail, width), 0)
+    is_mem = tail_row >= tail - mem_rows
+    init_b = jnp.where(is_mem, par[...], 0.0)
+    given = jnp.where(is_home, r_.memp[...].astype(F32), r_.memp_in[...].astype(F32))
+    first_b = jnp.where(flags[0] > 0, init_b, pltpu.roll(given, tail - mem_rows, 0))
+    r_.cur_b[...] = first_b.astype(BF)
+    r_.cur_a[...] = pltpu.roll(first_b, mem_rows, 0).astype(BF)
+
+    def take_rows(r):
+        inside = lax.broadcasted_iota(jnp.int32, (step, seg_len), 0)
+        nat = lax.broadcasted_iota(jnp.int32, (step, seg_len), 1)
+        return jnp.where((nat == r * text_rows + inside + mem_rows) & (inside < text_rows), 1.0, 0.0).astype(BF)
+
+    def place_rows(r):
+        nat = lax.broadcasted_iota(jnp.int32, (step, seg_len), 0) + r * step
+        pad = lax.broadcasted_iota(jnp.int32, (step, seg_len), 1)
+        inside = pad & (step - 1)
+        target = (pad // step) * text_rows + inside + mem_rows
+        return jnp.where((nat == target) & (inside < text_rows), 1.0, 0.0).astype(BF)
+
+    def exchange(slot, r):
+        return push(
+            r_.send_buf.at[slot, r], r_.recv_buf.at[slot, r], r_.send_sem.at[slot, r], r_.recv_sem.at[slot, r],
+            sibling,
+        )
+
+    def give(slot, r, part):
+        acc[rows(r), :] = part
+        r_.send_buf[slot, r] = part.astype(BF)
+        exchange(slot, r).start()
+
+    def taken(slot, r):
+        exchange(slot, r).wait()
+        return acc[rows(r), :] + r_.recv_buf[slot, r].astype(F32)
+
+    def back_copy(which, seg, zt):
+        src, dst = ((r_.y, r_.acts_o), (r_.text_all, r_.dt_all))[which]
+        span = pl.ds(pl.multiple_of(zt * step + core * piece, piece), piece)
+        return src.at[seg, span], dst.at[z % 2, seg, pl.ds(core * piece, piece)]
+
+    def back_out(which, seg, i):
+        zt = (z + i) % head_count
+        src, dst = back_copy(which, seg, zt)
+        return push(
+            src, dst, r_.back_s.at[which, seg, i], r_.back_r.at[which, seg, z % 2, core], device(z // 2, px, py, zt)
+        )
+
+    def back_here(which, seg):
+        src, dst = back_copy(which, seg, z)
+        return pltpu.make_async_copy(src, dst, r_.back_here_sem.at[which, seg])
+
+    def back_send(which, seg):
+        pl.when(is_home)(lambda: back_here(which, seg).start())
+        pl.when(away)(lambda: back_out(which, seg, 0).start())
+        for i in range(1, head_count):
+            back_out(which, seg, i).start()
+
+    def back_done(which, seg):
+        pl.when(is_home)(lambda: back_here(which, seg).wait())
+        pl.when(away)(lambda: back_out(which, seg, 0).wait_send())
+        for i in range(1, head_count):
+            back_out(which, seg, i).wait_send()
+        src, dst = ((r_.y, r_.acts_o), (r_.text_all, r_.dt_all))[which]
+        for j in range(2):
+            for h in range(2):
+                when_not(
+                    (core == h) & (z == 2 * core + j),
+                    lambda: push(
+                        src.at[seg, pl.ds(0, piece)], dst.at[j, seg, pl.ds(h * piece, piece)],
+                        r_.back_s.at[which, seg, 0], r_.back_r.at[which, seg, j, h], sibling,
+                    ).wait_recv(),
+                )
+
+    def build(seg):
+        def one(r):
+            x[seg, rows(r), :] = nn(place_rows(r), r_.text_all[seg]).astype(BF)
+
+        loop(head_count, one)
+        x[seg, 0:tail, :] = x[seg, 0:tail, :] + r_.cur_a[...]
+        x[seg, seg_len - tail : seg_len, :] = x[seg, seg_len - tail : seg_len, :] + r_.cur_b[...]
+        right = r_.seq[seg : seg + 1, :]
+        left = as_column(right)
+        acc[:, 0:seg_len] = jnp.where((left == right) | (left < 0) | (right < 0), 0.0, -1e30)
+
+    def project(seg):
+        def one(i):
+            j, t = i // 3, i % 3
+            at = pl.ds(pl.multiple_of(t * local, local), local)
+            value = nt(wa[j, at, :], x[seg]) + r_.bqv[j, at, :]
+            qkv[seg, j, at, :] = (value * jnp.where(t == 0, 0.125, 1.0)).astype(BF)
+
+        loop(6, one)
+
+    def attend(seg, first, count):
+        def one(i):
+            h = first + i
+            j = h // per_block
+            q, k, v = (qkv[seg, j, head_rows(h, part), :] for part in range(3))
+            s = tn(k, q) + acc[:, 0:seg_len]
+            e = jnp.exp(s - jnp.max(s, axis=0, keepdims=True))
+            p = (e * (1.0 / jnp.sum(e, axis=0, keepdims=True))).astype(BF)
+            pt[seg, h] = p
+            ot[seg, j, head_rows(h, 0), :] = nn(v, p).astype(BF)
+
+        loop(count, one)
+
+    def out_project(seg):
+        def one(r):
+            give(
+                0, r,
+                tn(ot[seg, 0, :, rows(r)], wa[0, 3 * local :, :]) + tn(ot[seg, 1, :, rows(r)], wa[1, 3 * local :, :]),
+            )
+
+        loop(head_count, one)
+
+    def norm_one(seg):
+        def one(r):
+            hat, scale = norm(x[seg, rows(r), :].astype(F32) + taken(0, r) + par[3:4, :])
+            r_.xh1[seg, rows(r), :] = hat.astype(BF)
+            r_.rs[rows(r), 2 * seg : 2 * seg + 1] = scale
+            h = hat * par[0:1, :] + par[2:3, :]
+            hf[rows(r), :] = h
+            r_.hb[seg, rows(r), :] = h.astype(BF)
+
+        loop(head_count, one)
+
+    def inner(seg, i):
+        v = nt(r_.hb[seg], wf[0, cols(i), :]) + r_.bin_row[:, cols(i)]
+        c0 = 0.7978845608028654
+        sq = v * v
+        th = jnp.tanh(v * (c0 + (c0 * 0.044715) * sq))
+        up = 0.5 + 0.5 * th
+        r_.u[seg, :, cols(i)] = (v * up).astype(BF)
+        slope = up + (0.5 * v) * (1.0 - th * th) * (c0 + (3 * c0 * 0.044715) * sq)
+        r_.gp[seg, :, cols(i)] = slope.astype(BF)
+
+    def outer(seg):
+        loop(head_count, lambda r: give(1, r, nn(r_.u[seg, rows(r), :], wf[1])))
+
+    def norm_two(seg):
+        def one(r):
+            hat, scale = norm(hf[rows(r), :] + taken(1, r) + par[4:5, :])
+            r_.xh2[seg, rows(r), :] = hat.astype(BF)
+            r_.rs[rows(r), 2 * seg + 1 : 2 * seg + 2] = scale
+            r_.y[seg, rows(r), :] = (hat * par[1:2, :] + par[5:6, :]).astype(BF)
+
+        loop(head_count, one)
+
+    def next_memory():
+        last = r_.y[0, seg_len - tail : seg_len, :].astype(F32)
+        memory = jnp.where(is_mem, jnp.where(flags[1] > 0, par[...], last), 0.0)
+        r_.cur_b[...] = memory.astype(BF)
+        r_.cur_a[...] = pltpu.roll(memory, mem_rows, 0).astype(BF)
+
+    rows_ready(0)
+    build(0)
+    ffn_one(1)
+    for k in range(2):
+
+        def last_part():
+            attention_plane(k, 2).wait_recv()
+            attention_plane(k, 3).wait_recv()
+
+        pl.when(foreign[k])(last_part)
+
+    def kept_own():
+        for copy in own_attention:
+            copy.wait()
+
+    pl.when(is_home)(kept_own)
+    project(0)
+    ffn_one(2)
+    attend(0, 0, 2)
+    ffn_two(1)
+    attend(0, 2, 2)
+    ffn_one(3)
+    rows_send(1)
+    attend(0, 4, heads - 4)
+    out_project(0)
+    ffn_two(2)
+    norm_one(0)
+    for n in range(2):
+        ffn_ready(n)
+        inner(0, order[n])
+    ffn_two(3)
+    for n in range(2, head_count):
+        ffn_ready(n)
+        inner(0, order[n])
+    outer(0)
+    rows_pass(1)
+    rows_done(0)
+    rows_send(3)
+    rows_send(2)
+    norm_two(0)
+    next_memory()
+    back_send(0, 0)
+
+    rows_ready(1)
+    build(1)
+    project(1)
+    attend(1, 0, heads)
+    rows_pass(3)
+    rows_done(1)
+    out_project(1)
+    norm_one(1)
+    loop(head_count, lambda i: inner(1, i))
+    rows_pass(2)
+    outer(1)
+    norm_two(1)
+    back_send(0, 1)
+    rows_ready(3)
+    rows_ready(2)
+
+    def pull_two(seg):
+        def one(r):
+            g_y = r_.cot_all[seg, rows(r), :].astype(F32)
+            if seg == 0:
+                g_y = g_y + jnp.where(r == head_count - 1, r_.carry[...], 0.0)
+            hat = r_.xh2[seg, rows(r), :].astype(F32)
+            pre = pull_norm(g_y * par[1:2, :], hat, r_.rs[rows(r), 2 * seg + 1 : 2 * seg + 2])
+            hf[rows(r), :] = pre
+            r_.xh2[seg, rows(r), :] = pre.astype(BF)
+            r_.sg[1:2, :] += row_sum(g_y * hat)
+            r_.sg[5:6, :] += row_sum(g_y)
+            r_.sg[4:5, :] += row_sum(pre)
+
+        loop(head_count, one)
+
+    def pull_inner(seg, i):
+        g_u = nt(r_.xh2[seg], wf[1, cols(i), :])
+        g_z = (g_u * r_.gp[seg, :, cols(i)].astype(F32)).astype(BF)
+        r_.gp[seg, :, cols(i)] = g_z
+        r_.dbin[0:1, cols(i)] += row_sum(g_z.astype(F32))
+
+    def pull_hidden(seg):
+        loop(head_count, lambda r: give(0, r, nn(r_.gp[seg, rows(r), :], wf[0])))
+
+    def pull_one(seg):
+        def one(r):
+            g_h = hf[rows(r), :] + taken(0, r)
+            hat = r_.xh1[seg, rows(r), :].astype(F32)
+            pre = pull_norm(g_h * par[0:1, :], hat, r_.rs[rows(r), 2 * seg : 2 * seg + 1])
+            hf[rows(r), :] = pre
+            r_.xh1[seg, rows(r), :] = pre.astype(BF)
+            r_.sg[0:1, :] += row_sum(g_h * hat)
+            r_.sg[2:3, :] += row_sum(g_h)
+            r_.sg[3:4, :] += row_sum(pre)
+
+        loop(head_count, one)
+
+        def out(j):
+            r_.got[j] = nt(wa[j, 3 * local :, :], r_.xh1[seg]).astype(BF)
+
+        loop(2, out)
+
+    def pull_heads(seg, first, count):
+        def one(i):
+            h = first + i
+            j = h // per_block
+            q, k, v = (qkv[seg, j, head_rows(h, part), :] for part in range(3))
+            g_o = r_.got[j, head_rows(h, 0), :]
+            p = pt[seg, h]
+            d_v = nt(g_o, p).astype(BF)
+            total_p = row_sum(g_o.astype(F32) * ot[seg, j, head_rows(h, 0), :].astype(F32))
+            d_s = (p.astype(F32) * (tn(v, g_o) - total_p)).astype(BF)
+            d_q = (nn(k, d_s) * 0.125).astype(BF)
+            d_k = nt(q, d_s).astype(BF)
+            for part, value in enumerate((d_q, d_k, d_v)):
+                qkv[seg, j, head_rows(h, part), :] = value
+
+        loop(count, one)
+
+    def pull_rows(seg):
+        def one(r):
+            give(
+                1, r,
+                tn(qkv[seg, 0, :, rows(r)], wa[0, : 3 * local, :]) + tn(qkv[seg, 1, :, rows(r)], wa[1, : 3 * local, :]),
+            )
+
+        loop(head_count, one)
+
+    def pull_x(seg):
+        def one(r):
+            value = hf[rows(r), :] + taken(1, r)
+            acc[rows(r), :] = value
+            r_.send_buf[1, r] = value.astype(BF)
+
+        loop(head_count, one)
+        both = pltpu.roll(acc[0:tail, :], tail - mem_rows, 0) + acc[seg_len - tail : seg_len, :]
+        memory = jnp.where(is_mem, both, 0.0)
+        r_.dinit[...] += jnp.where(flags[seg] > 0, memory, 0.0)
+        if seg == 1:
+            r_.carry[step - tail : step, :] = jnp.where(flags[1] > 0, 0.0, memory)
+
+    def text_grad(seg):
+        def one(r):
+            r_.text_all[seg, rows(r), :] = nn(take_rows(r), r_.send_buf[1].reshape(seg_len, width)).astype(BF)
+
+        loop(head_count, one)
+
+    pull_two(1)
+    loop(head_count, lambda i: pull_inner(1, i))
+    pull_hidden(1)
+    pull_one(1)
+    pull_heads(1, 0, heads)
+    pull_rows(1)
+    pull_x(1)
+    text_grad(1)
+    back_send(1, 1)
+
+    def cut(buf, kind, a, b):
+        first, second = (px, py) if kind == 0 else (py, px)
+        first = first if a == 0 else 1 - first
+        second = second if b == 0 else 1 - second
+        return buf.at[second, first] if kind == 0 else buf.at[first, second]
+
+    sum_mates = ((x_mate, y_mate), (y_mate, x_mate))
+
+    def sum_one(name, kind, b):
+        buf, got, s, r = sums[name](kind)
+        return push(cut(buf, kind, 1, b), got[0].at[b], s.at[b], r.at[b], sum_mates[kind][0])
+
+    def sum_two(name, kind):
+        buf, got, s, r = sums[name](kind)
+        return push(cut(buf, kind, 0, 1), got[1], s.at[2], r.at[2], sum_mates[kind][1])
+
+    def ffn_sum(d):
+        zi = (z + d) % head_count
+
+        def parts(kind):
+            return (
+                r_.fsend.at[kind, zi], (r_.f_one.at[kind, zi], r_.f_two.at[kind, zi]),
+                r_.fsum_s.at[kind, zi], r_.fsum_r.at[kind, zi],
+            )
+
+        return parts
+
+    sums = {d: ffn_sum(d) for d in range(head_count)}
+    sums["a"] = lambda kind: (
+        r_.asend.at[kind], (r_.a_one.at[kind], r_.a_two.at[kind]), r_.asum_s.at[kind], r_.asum_r.at[kind]
+    )
+    sums["v"] = lambda kind: (
+        r_.vsend.at[kind], (r_.v_one.at[kind], r_.v_two.at[kind]), r_.vsum_s.at[kind], r_.vsum_r.at[kind]
+    )
+
+    def start_sum(name):
+        for b in (1, 0):
+            for kind in range(2):
+                sum_one(name, kind, b).start()
+
+    def adder(name):
+        return add_block if isinstance(name, int) else add_blocks
+
+    def go_on(name):
+        for kind in range(2):
+            buf, got, _, _ = sums[name](kind)
+            sum_one(name, kind, 1).wait_recv()
+            adder(name)(cut(buf, kind, 0, 1), got[0].at[1])
+            sum_two(name, kind).start()
+        for kind in range(2):
+            buf, got, _, _ = sums[name](kind)
+            sum_one(name, kind, 0).wait_recv()
+            adder(name)(cut(buf, kind, 0, 0), got[0].at[0])
+
+    def end_plane(name):
+        for kind in range(2):
+            buf, got, _, _ = sums[name](kind)
+            sum_two(name, kind).wait_recv()
+            adder(name)(cut(buf, kind, 0, 0), got[1])
+
+    def sum_sent(name):
+        for kind in range(2):
+            for b in range(2):
+                sum_one(name, kind, b).wait_send()
+            sum_two(name, kind).wait_send()
+
+    def z_out(kind, d):
+        zi = (z + d) % head_count
+        return push(
+            cut(r_.fsend.at[kind, zi], kind, 0, 0), r_.f_z.at[kind, z], r_.fz_s.at[kind, d], r_.fz_r.at[kind, z],
+            device(core, px, py, zi),
+        )
+
+    def z_in(kind, zs):
+        return push(
+            cut(r_.fsend.at[kind, z], kind, 0, 0), r_.f_z.at[kind, zs], r_.fz_s.at[kind, 0], r_.fz_r.at[kind, zs], sibling
+        )
+
+    def end_ffn(d):
+        end_plane(d)
+        if d > 0:
+            for kind in range(2):
+                z_out(kind, d).start()
+
+    def last_out(name, k, h):
+        buf, dst, s, r = last[name]
+        return push(
+            cut(buf.at[k], k, 0, 0).at[h], dst.at[z], s.at[k, h], r.at[z], device(h, px, py, 2 * core + k)
+        )
+
+    def last_here(name, k):
+        buf, dst, _, _ = last[name]
+        return pltpu.make_async_copy(cut(buf.at[k], k, 0, 0).at[core], dst.at[z], r_.last_sem.at["av".index(name)])
+
+    last = {
+        "a": (r_.asend, r_.a_z, r_.az_s, r_.az_r),
+        "v": (r_.vsend, r_.v_z, r_.vz_s, r_.vz_r),
+    }
+
+    def last_each(name, here_do, away_do):
+        for k in range(2):
+            for h in range(2):
+                here = (core == h) & (z == 2 * core + k)
+                if here_do is not None:
+                    pl.when(here)(lambda: here_do(last_here(name, k)))
+                when_not(here, lambda: away_do(last_out(name, k, h)))
+
+    def last_total(name):
+        buf, dst, s, r = last[name]
+        for zs in range(head_count):
+            here = is_home & (z == zs)
+            pl.when(here)(lambda: last_here(name, 0).wait())
+            when_not(
+                here, lambda: push(buf.at[0, 0, 0, 0], dst.at[zs], s.at[0, 0], r.at[zs], sibling).wait_recv()
+            )
+        value = dst[0].astype(F32)
+        for zs in range(1, head_count):
+            value = value + dst[zs].astype(F32)
+        return value
+
+    def ffn_grads(d):
+        i = (z + d) % head_count
+        pull_inner(0, i)
+        for kind, (left, right) in enumerate(((r_.gp, r_.hb), (r_.u, r_.xh2))):
+            value = tn(left[0, :, cols(i)], right[0]) + tn(left[1, :, cols(i)], right[1])
+            for p in range(planes):
+                r_.fsend[kind, i, p // 2, p % 2] = value[p * hid : (p + 1) * hid, :].astype(BF)
+        start_sum(d)
+
+    pull_two(0)
+    ffn_grads(1)
+    ffn_grads(2)
+    go_on(1)
+    ffn_grads(3)
+    go_on(2)
+    end_ffn(1)
+    ffn_grads(0)
+    dbin_pair = push(r_.dbin, r_.dbin_in, r_.pair_s.at[2], r_.pair_r.at[2], sibling)
+    dbin_pair.start()
+    pull_hidden(0)
+    go_on(3)
+    end_ffn(2)
+    pull_one(0)
+    pull_heads(0, 0, 3)
+    go_on(0)
+    end_ffn(3)
+    pull_heads(0, 3, heads - 3)
+    end_ffn(0)
+
+    def attention_grads(i):
+        wide = width // 2
+        span = pl.ds(pl.multiple_of(i * wide, wide), wide)
+        xt = [x[s, :, span].T for s in range(2)]
+        gt = [r_.xh1[s, :, span].T for s in range(2)]
+        part = hid_rows
+        for k in range(2):
+            qkv_g = nt(xt[0], qkv[0, k]) + nt(xt[1], qkv[1, k])
+            out_g = nt(gt[0], ot[0, k]) + nt(gt[1], ot[1, k])
+            for b in range(4):
+                at = slice(b * part, (b + 1) * part)
+                r_.asend[k, i, b // 2, b % 2, :, 0 : 3 * local] = qkv_g[at, :].astype(BF)
+                r_.asend[k, i, b // 2, b % 2, :, 3 * local :] = out_g[at, :].astype(BF)
+
+    hid_rows = width // dp_count
+    attention_grads(1 - py)
+    attention_grads(py)
+    start_sum("a")
+    pull_rows(0)
+    pull_x(0)
+    text_grad(0)
+    back_send(1, 0)
+    dbin_pair.wait()
+
+    dbin_both = [jnp.where(core == h, r_.dbin[0:1, :], r_.dbin_in[0:1, :]) for h in range(2)]
+    for k in range(2):
+        r_.bqv[k] = sum(jnp.sum(qkv[s, k].astype(F32), axis=1, keepdims=True) for s in range(2))
+    sg, dinit = r_.sg, r_.dinit
+    r_.vec[...] = jnp.where(is_mem, dinit[...], 0.0)
+    r_.vec[0:6, :] = sg[0:6, :]
+    vtmp[...] = jnp.zeros_like(vtmp)
+
+    def by_core(cut_of):
+        return jnp.where(core == 0, cut_of(0), cut_of(1))
+
+    qv_rows = [
+        [
+            jnp.sum(
+                jnp.where(
+                    lax.broadcasted_iota(jnp.int32, (HD, HD), 0) == lax.broadcasted_iota(jnp.int32, (HD, HD), 1),
+                    r_.bqv[k, 2 * part * local + b * HD : 2 * part * local + (b + 1) * HD, :],
+                    0.0,
+                ),
+                axis=0,
+                keepdims=True,
+            )
+            for part in range(2)
+            for b in range(per_block)
+        ]
+        for k in range(2)
+    ]
+    piece_b = HD // dp_count
+    vec = r_.vec[...]
+
+    def small_cut(k, p, h):
+        dp_t = 2 * p + h
+
+        def from_vec(c):
+            at = (dp_t * head_count + 2 * c + k) * lanes
+            return vec[:, at : at + lanes]
+
+        def from_bin(c):
+            at = ((2 * c + k) * planes + p) * hid
+            return dbin_both[h][:, at : at + hid]
+
+        vtmp[0:16, 0:lanes] = by_core(from_vec)
+        vtmp[0:1, 32 : 32 + hid] = by_core(from_bin)
+        for n, line in enumerate(qv_rows[k]):
+            vtmp[1:2, 32 + n * piece_b : 32 + (n + 1) * piece_b] = line[:, dp_t * piece_b : (dp_t + 1) * piece_b]
+        r_.vsend[k, p // 2, p % 2, h] = vtmp[...].astype(BF)
+
+    for k in range(2):
+        for p in range(planes):
+            for h in range(2):
+                small_cut(k, p, h)
+    start_sum("v")
+    go_on("a")
+    go_on("v")
+    end_plane("a")
+    last_each("a", lambda c: c.start(), lambda c: c.start())
+    end_plane("v")
+    last_each("v", lambda c: c.start(), lambda c: c.start())
+
+    for kind, out in enumerate((r_.win_o, r_.wback_o)):
+        value = cut(r_.fsend.at[kind, z], kind, 0, 0)[...].astype(F32)
+        for d in range(1, head_count):
+            zs = (z + d) % head_count
+            z_in(kind, zs).wait_recv()
+            value = value + r_.f_z[kind, zs].astype(F32)
+        out[...] = value
+    r_.att_o[...] = last_total("a")
+    r_.vec_o[...] = last_total("v")
+
+    for name in (0, 1, 2, 3, "a", "v"):
+        sum_sent(name)
+    for d in range(1, head_count):
+        for kind in range(2):
+            z_out(kind, d).wait_send()
+    for name in "av":
+        last_each(name, None, lambda c: c.wait_send())
+    for which in range(2):
+        for seg in range(2):
+            back_done(which, seg)
+    for a in range(2, 4):
+        rows_done(a)
+    attention_outs(lambda c: c.wait_send())
+    ffn_sent()
+    for copy in pair:
+        copy.wait_send()
+    for k in range(2):
+
+        def sent():
+            for which in range(4):
+                attention_plane(k, which).wait_send()
+
+        pl.when(foreign[k])(sent)
+    for zi in range(head_count):
+        for kind in range(2):
+            for which in range(3):
+                side(kind, zi, which).wait_send()
+    for i in range(column_size):
+        small_out(i).wait_send()
+    for i in range(3):
+        small_plane(i).wait_send()
+    r_.dt_o[...] = r_.dt_all[...]
+
+
+def vmem(*shape, dtype=BF):
+    return pltpu.VMEM(shape, dtype)
+
+
+def f32(*shape):
+    return pltpu.VMEM(shape, F32)
+
+
+def sds(*shape, dtype=BF):
+    return jax.ShapeDtypeStruct(shape, dtype)
+
+
+def dma(*shape):
+    return pltpu.SemaphoreType.DMA(shape)
+
+
+ANY = pl.BlockSpec(memory_space=pl.ANY)
+INV = pl.BlockSpec(memory_space=pltpu.VMEM)
+INS = pl.BlockSpec(memory_space=pltpu.SMEM)
+
+
+def end_kernel(mem_rows, hid, lanes, acts, dt, win, wback, att, vec, *outs):
+    acts_o, dt_o, dinit_o, dqkv_o, dbqv_o, dwout_o, dwin_o, dwback_o, dbin_o, dgains_o, dbiases_o = outs
+    acts_o[...] = acts[...]
+    text_rows = dt_o.shape[2]
+    for j in range(2):
+        for s in range(2):
+            dt_o[j, s] = dt[j, s, 0:text_rows, :]
+    dinit_o[...] = vec[6 : 6 + mem_rows, 0:lanes]
+    parts, _, local_width = dqkv_o.shape
+    for t in range(parts):
+        dqkv_o[t] = att[:, t * local_width : (t + 1) * local_width]
+    per_block, _, slice_b = dbqv_o.shape
+    for b in range(per_block):
+        for part in range(2):
+            at = 32 + (part * per_block + b) * slice_b
+            dbqv_o[b, part : part + 1, :] = vec[1:2, at : at + slice_b]
+    dwout_o[...] = att[:, parts * local_width :].T
+    dwin_o[...] = win[...]
+    dwback_o[...] = wback[...]
+    dbin_o[...] = vec[0:1, 32 : 32 + hid]
+    dgains_o[...] = vec[0:2, 0:lanes]
+    dbiases_o[...] = vec[2:6, 0:lanes]
+
+
+def by_chip(
+    text, boundary, reset, memory_in, init_memory, w_qkv, b_qv, w_out, w_in, w_back, b_in, norm_gains, biases,
+    cotangent,
+):
+    head_count = lax.axis_size("head")
+    dp_count = lax.axis_size("dp")
+    planes = dp_count // 2
+    total = dp_count * head_count
+    text_rows, width = text.shape[2], text.shape[3]
+    block = cotangent.shape[2]
+    seg_len = block * head_count
+    mem_rows = memory_in.shape[1]
+    local = w_qkv.shape[2]
+    hid = w_in.shape[1]
+    lanes = norm_gains.shape[1]
+    heads = 2 * local // HD
+    hidden = hid * planes * head_count
+    share = width // dp_count
+
+    inputs = dict(
+        text=(text, INV),
+        boundary=(boundary, INV),
+        reset=(reset, INS),
+        memory_in=(memory_in.transpose(1, 0, 2), INV),
+        init_memory=(init_memory, INV),
+        wq_t=(w_qkv.transpose(1, 2, 0).reshape(3 * local, width), ANY),
+        w_out=(w_out, ANY),
+        b_qv=(b_qv.transpose(1, 0, 2), INV),
+        w_in_t=(w_in.T, INV),
+        w_back=(w_back, INV),
+        b_in=(b_in[None, :], INV),
+        norm_gains=(norm_gains, INV),
+        biases=(biases, INV),
+        cotangent=(cotangent, ANY),
+    )
+    outputs = dict(
+        acts_o=(sds(2, 2, block, width), ANY),
+        dt_o=(sds(2, 2, block, width), INV),
+        win_o=(sds(hid, width, dtype=F32), INV),
+        wback_o=(sds(hid, width, dtype=F32), INV),
+        att_o=(sds(share, width, dtype=F32), INV),
+        vec_o=(sds(16, 128, dtype=F32), INV),
+    )
+    scratch = dict(
+        text_pad=vmem(2, 2, block, width),
+        text_all=vmem(2, seg_len, width),
+        cot_all=vmem(2, seg_len, width),
+        wa=vmem(2, 4 * local, width),
+        wf=vmem(2, hidden, width),
+        small=vmem(16, 128),
+        small_all=vmem(total, 16, 128),
+        seqf=f32(8, seg_len),
+        seqf_in=f32(8, seg_len),
+        seq=f32(8, seg_len),
+        memp=vmem(16, width),
+        memp_in=vmem(16, width),
+        par=f32(16, width),
+        bin_row=f32(1, hidden),
+        bqv=f32(2, 3 * local, 1),
+        x=vmem(2, seg_len, width),
+        qkv=vmem(2, 2, 3 * local, seg_len),
+        pt=vmem(2, heads, seg_len, seg_len),
+        ot=vmem(2, 2, local, seg_len),
+        hf=f32(seg_len, width),
+        acc=f32(seg_len, width),
+        xh1=vmem(2, seg_len, width),
+        hb=vmem(2, seg_len, width),
+        u=vmem(2, seg_len, hidden),
+        gp=vmem(2, seg_len, hidden),
+        xh2=vmem(2, seg_len, width),
+        rs=f32(seg_len, 4),
+        y=vmem(2, seg_len, width),
+        got=vmem(2, local, seg_len),
+        send_buf=vmem(2, head_count, block, width),
+        recv_buf=vmem(2, head_count, block, width),
+        cur_a=vmem(16, width),
+        cur_b=vmem(16, width),
+        carry=f32(block, width),
+        sg=f32(8, width),
+        dinit=f32(16, width),
+        dbin=f32(8, hidden),
+        dbin_in=f32(8, hidden),
+        vec=f32(16, width),
+        vtmp=f32(16, 128),
+        dt_all=vmem(2, 2, block, width),
+        fsend=vmem(2, head_count, 2, 2, hid, width),
+        f_one=vmem(2, head_count, 2, hid, width),
+        f_two=vmem(2, head_count, hid, width),
+        f_z=vmem(2, head_count, hid, width),
+        asend=vmem(2, 2, 2, 2, share, width),
+        a_one=vmem(2, 2, 2, share, width),
+        a_two=vmem(2, 2, share, width),
+        a_z=vmem(head_count, share, width),
+        vsend=vmem(2, 2, 2, 2, 16, 128),
+        v_one=vmem(2, 2, 2, 16, 128),
+        v_two=vmem(2, 2, 16, 128),
+        v_z=vmem(head_count, 16, 128),
+        small_s=dma(7),
+        small_r=dma(4, 2),
+        small_ps=dma(3),
+        small_pr=dma(3),
+        pair_s=dma(3),
+        pair_r=dma(3),
+        att_s=dma(3),
+        att_r=dma(2, 2),
+        plane_s=dma(2, 4),
+        plane_r=dma(2, 4),
+        local_sem=dma(2),
+        rows_s=dma(4, 2, 2),
+        rows_r=dma(4, 4),
+        here_sem=dma(4),
+        fwd_s=dma(4, 4),
+        fwd_r=dma(4, 4),
+        ffn_s=dma(5),
+        ffn_r=dma(4),
+        side_s=dma(4, 2, 3),
+        side_r=dma(4, 2, 3),
+        send_sem=dma(2, 4),
+        recv_sem=dma(2, 4),
+        back_s=dma(2, 2, 4),
+        back_r=dma(2, 2, 2, 2),
+        back_here_sem=dma(2, 2),
+        fsum_s=dma(2, 4, 3),
+        fsum_r=dma(2, 4, 3),
+        asum_s=dma(2, 3),
+        asum_r=dma(2, 3),
+        vsum_s=dma(2, 3),
+        vsum_r=dma(2, 3),
+        fz_s=dma(2, 4),
+        fz_r=dma(2, 4),
+        az_s=dma(2, 2),
+        az_r=dma(4),
+        vz_s=dma(2, 2),
+        vz_r=dma(4),
+        last_sem=dma(2),
+    )
+    names = tuple(inputs) + tuple(outputs) + tuple(scratch)
+    middle = pl.pallas_call(
+        functools.partial(main_kernel, names, dp_count, head_count),
+        out_shape=tuple(v[0] for v in outputs.values()),
+        in_specs=[v[1] for v in inputs.values()],
+        out_specs=tuple(v[1] for v in outputs.values()),
+        scratch_shapes=list(scratch.values()),
+        compiler_params=pltpu.CompilerParams(
+            collective_id=0, has_side_effects=True, vmem_limit_bytes=VMEM_LIMIT
+        ),
+        name="layer",
+    )(*(v[0] for v in inputs.values()))
+
+    slice_b = HD // dp_count
+    out = pl.pallas_call(
+        functools.partial(end_kernel, mem_rows, hid, lanes),
+        out_shape=(
+            sds(2, 2, block, width),
+            sds(2, 2, text_rows, width),
+            sds(mem_rows, lanes, dtype=F32),
+            sds(3, share, local, dtype=F32),
+            sds(local // HD, 2, slice_b, dtype=F32),
+            sds(local, share, dtype=F32),
+            sds(hid, width, dtype=F32),
+            sds(hid, width, dtype=F32),
+            sds(1, hid, dtype=F32),
+            sds(2, lanes, dtype=F32),
+            sds(4, lanes, dtype=F32),
+        ),
+        in_specs=[INV] * 6,
+        out_specs=tuple([INV] * 11),
+        name="results",
+    )(*middle)
+    acts, d_text, d_init, d_qkv, d_bqv, d_wout, d_win, d_wback, d_bin, d_gains, d_biases = out
+    return (
+        acts, d_text, d_init,
+        d_qkv.transpose(1, 0, 2),
+        d_bqv.transpose(1, 0, 2),
+        d_wout, d_win.T, d_wback, d_bin[0], d_gains, d_biases,
+    )
+
+
 def solution(mesh):
+    body = by_chip if mesh.shape["dp"] == 8 and mesh.shape["head"] == 4 else local
     return jax.shard_map(
-        local,
+        body,
         mesh=mesh,
         in_specs=(
             P("dp", None, "head", None),

time: 1050 us -> 222 us (0.21)
  waiting for transfers between devices: 478 us -> 0 us
  blocking collectives: 323 us -> 0 us
  Pallas kernels: 0 us -> 216 us
  matrix products: 98.1 us -> 0 us
  local copies, waits for them, and re-layouts: 75 us -> 4.87 us
  other arithmetic: 47.8 us -> 0 us
  between operations: 20.2 us -> 0.65 us
    reduce_scatter x7 -> x0, waiting for transfers between devices: 263 us -> none  [the longest x1 85 us: local(): lax.psum_scatter(ffn_total[0].astype(jnp.bfloat16), 'head', scatter_dimen...]
    pallas_call x0 -> x2, Pallas kernels: none -> 216 us  [the longest x1 212 us: by_chip(): pl.pallas_call(functools.partial(main_kernel, names, dp_count, head_count...]
    all_gather x3 -> x0, blocking collectives: 202 us -> none  [the longest x1 73 us: local(): lax.all_gather(init_memory, ('dp', 'head'), axis=1, tiled=True)]
    unnamed x23 -> x0, waiting for transfers between devices: 180 us -> none
    dot_general x36 -> x0, matrix products: 98.1 us -> none  [the longest x2 10.7 us: backward(): jnp.einsum('srd,fd->srf', grad_outer, w_back_all, preferred_element_type=...]
    unnamed x2 -> x0, blocking collectives: 62.3 us -> none
    psum x3 -> x0, blocking collectives: 58.2 us -> none  [the longest x2 39.8 us: backward(): lax.psum((grad_rows[:, :mem_rows] + grad_rows[:, seg_len - mem_rows:]).as...]
    all_gather x6 -> x0, waiting for transfers between devices: 34.5 us -> none  [the longest x2 34.4 us: backward(): lax.all_gather(grad_pre.astype(jnp.bfloat16), 'head', axis=1, tiled=True)]
  transfers between devices with their start and end apart: 18 -> 0, of which waited for: 12 -> 0; matrix products, arithmetic and copies ran while one was open for 13% -> 0% of each run, Pallas kernels for 0% -> 0%
where the time goes in v2:
time: 222 us; the launch traced here: 221 us
  Pallas kernels  216 us (97%)
  local copies, waits for them, and re-layouts  4.87 us (2%)
    pallas_call x1, Pallas kernels, by_chip(): pl.pallas_call(functools.partial(main_kernel, names, dp_count, head_count...  212 us
    unnamed x2, local copies, waits for them, and re-layouts  4.87 us

profile of v2, /device:TPU:0, one launch (start us, length us, event | category | flops | bytes accessed | tf_op | source)
XLA Modules:
  0.0 221.2 jit_solution(17220274030082178043)
XLA Ops:
  0.6 2.1 copy.25.values_0_
  2.7 212.4 %layer.1 = (bf16[2,2,128,768]{3,2,1,0:T(8,128)(2,1)}, bf16[2,2,128,768]{3,2,1,0:T(8,128)(2,1)}, f32[96,768]{1,0:T(8,128)}, f32[96,768]{1,0:T(8,128)}, f32[96,768]{1,0:T(8,128)}, /*index=5*/f32[16,128]{1,0:T(8,128)}) custom-call(bf16[2,2,123,768]{3,2,1,0:T(8,128)(2,1)} %copy.25.values_0_, s32[2,2,492]{2,1,0:T(2,128)} %values_1_.1, s32[2,2]{1,0:T(2,128)} %values_2_.1, ...), custom_call_target="tpu_custom_call" | custom-call | tf_op jit(solution)/shard_map/layer/pallas_call | solution.py:1518
  215.2 3.3 %results.1 = (bf16[2,2,128,768]{3,2,1,0:T(8,128)(2,1)}, bf16[2,2,123,768]{3,2,1,0:T(8,128)(2,1)}, f32[10,24]{1,0:T(8,128)}, f32[3,96,192]{2,1,0:T(8,128)}, f32[3...) custom-call(bf16[2,2,128,768]{3,2,1,0:T(8,128)(2,1)} %get-tuple-elem, ...), custom_call_target="tpu_custom_call" | custom-call | tf_op jit(solution)/shard_map/results/pallas_call | solution.py:1531
  218.4 2.8 %copy.26 = bf16[2,2,123,768]{3,1,2,0:T(2,128)(2,1)} copy(bf16[2,2,123,768]{3,2,1,0:T(8,128)(2,1)} %get-tuple-element.46) | data formatting | bytes 1511424
